TPU v7x, 1024 devices: a whole 8x8x8 slice. The times are simulated.
1024 devices in a mesh: cross: 16 (over z, y_lo), node: 64 (over y_hi, x, core).
Axes of the slice: x: 8, y: 8 (y_hi: 4, y_lo: 2; y = y_hi * 2 + y_lo), z: 8, core: 2. Of those that a mesh axis runs over, the one named last changes fastest.
Arguments:
- tokens: bfloat16 [131072, 12288], P(('cross', 'node')), may hold values from -24 to 24
- codes: bfloat16 [64, 12288], P(None, 'node'), may hold values from -0.0546875 to 0.0546875
- code_scale: float32 [1, 384], P(None, 'node'), may hold values from 0.25 to 4
- upstream: bfloat16 [131072, 64], P(('cross', 'node')), may hold values from -0.0390625 to 0.0390625
Outputs:
- values: bfloat16 [131072, 64], P(('cross', 'node'))
- weight_grad: float32 [12288, 64], P(('cross', 'node'))
All inputs are finite; a program needn't handle non-finite values. Where the computation divides by a largest or mean magnitude, that divisor is 1e-20 or more.
Results may differ from a plain program's by a relative error of at most 0.015.
Values may be sent and summed in bfloat16 or wider, within the bound.
No kernel may reach another device: no remote copies, remote signals or barrier semaphores. Data moves between devices by JAX's collectives and lax.ppermute only.
A program may use at most 64 MiB of HBM per device.

v0:
```python
import jax
import jax.numpy as jnp
from jax import lax
from jax.sharding import PartitionSpec as P


def shards(tokens, codes, code_scale, upstream):
    width = tokens.shape[1]
    channels = upstream.shape[1]
    span = 2048 // channels
    piece_codes = lax.all_gather(codes, "node", axis=1, tiled=True)
    piece_scale = lax.all_gather(
        code_scale.astype(jnp.bfloat16), "node", axis=1, tiled=True
    ).astype(jnp.float32)
    columns = piece_codes.shape[1]
    nblocks = piece_scale.shape[1]
    scaled = piece_codes.astype(jnp.float32).reshape(channels, nblocks, columns // nblocks)
    scaled = scaled * piece_scale.reshape(1, nblocks, 1)
    weights = scaled.reshape(channels, columns).astype(jnp.bfloat16)
    projected = lax.dot_general(
        tokens, weights, (((1,), (1,)), ((), ())), preferred_element_type=jnp.float32
    )
    values = projected.astype(jnp.bfloat16)
    term = lax.dot_general(
        tokens, upstream, (((0,), (0,)), ((), ())), preferred_element_type=jnp.float32
    )
    blocks = term.reshape(width // span, span * channels)
    scale = jnp.max(jnp.abs(blocks), axis=1, keepdims=True) + 1e-06
    packed = (blocks / scale).astype(jnp.bfloat16)
    row_scale = jnp.broadcast_to(scale, (width // span, span)).reshape(width)
    n_cross = lax.axis_size("cross")
    n_node = lax.axis_size("node")
    own_rows = width // (n_cross * n_node)
    packed4 = packed.reshape(n_cross, n_node, own_rows, channels)
    scale3 = row_scale.reshape(n_cross, n_node, own_rows)
    got_packed, got_scale = (
        lax.all_to_all(packed4, "node", split_axis=1, concat_axis=1, tiled=True),
        lax.all_to_all(
            scale3.astype(jnp.bfloat16), "node", split_axis=1, concat_axis=1, tiled=True
        ).astype(scale3.dtype),
    )
    partial_sum = jnp.sum(got_packed.astype(jnp.float32) * got_scale[..., None], axis=1)
    arrived = lax.all_to_all(
        partial_sum.astype(jnp.bfloat16), "cross", split_axis=0, concat_axis=0, tiled=True
    ).astype(partial_sum.dtype)
    weight_grad = jnp.sum(arrived, axis=0)
    return (values, weight_grad)


def solution(mesh):
    in_specs = (
        P(("cross", "node"), None),
        P(None, "node"),
        P(None, "node"),
        P(("cross", "node"), None),
    )
    out_specs = (P(("cross", "node"), None), P(("cross", "node"), None))
    return jax.shard_map(shards, mesh=mesh, in_specs=in_specs, out_specs=out_specs, check_vma=False)
```

profile of v0, /device:TPU:1, one launch (start us, length us, event | category | flops | bytes accessed | tf_op | source)
XLA Modules:
  0.0 293.6 jit_solution(12407479330393017653)
XLA Ops:
  7.2 1.9 copy-done
  9.1 3.0 %abs_reduce_fusion = (f32[12288]{0:T(1024)S(1)}, f32[12288,64]{0,1:T(8,128)}) fusion(bf16[128,64]{0,1:T(8,128)(2,1)} %param.7, bf16[128,12288]{1,0:T(8,128)(2,1)S(1)} %copy-done), kind=kOutput, calls=%fused_computation.3 | convolution fusion | flops 202887168 | bytes 6356992 | tf_op jit(solution)/shard_map/dot_general | solution.py:24
  12.0 0.1 reduce_max.14
  12.1 0.1 reduce_max.18
  12.3 0.1 div.13
  12.4 1.0 div.14
  13.5 1.1 convert_element_type.42
  14.5 0.9 copy.27
  15.4 18.2 %all-to-all-start.1 = ((bf16[16,64,12]{2,0,1:T(8,128)(2,1)}), bf16[16,64,12]{2,0,1:T(8,128)(2,1)S(1)}, u32[]{:S(2)}, u32[]{:S(2)}) async-start(bf16[16,64,12]{2,0,1:T(8,128)(2,1)} %copy.27), calls=%async_computation.1 | async-start | bytes 524288 | tf_op jit(solution)/shard_map/all_to_all | solution.py:38
  33.6 5.8 %copy.25 = f32[12288,64]{1,0:T(8,128)} copy(f32[12288,64]{0,1:T(8,128)} %get-tuple-element.3) | data formatting | bytes 6291456 | tf_op jit(solution)/shard_map/dot_general | solution.py:24
  39.4 8.2 %reshape.21 = f32[16,64,12,64]{3,2,1,0:T(8,128)} reshape(f32[12288,64]{1,0:T(8,128)} %copy.25) | data formatting | bytes 6291456 | tf_op jit(solution)/shard_map/reshape | solution.py:27
  47.7 5.3 %divide_convert_fusion = bf16[16,64,12,64]{3,2,1,0:T(8,128)(2,1)S(1)} fusion(f32[16,64,12,64]{3,2,1,0:T(8,128)} %reshape.21, f32[16,64,12]{2,1,0:T(8,128)} %div.14), kind=kLoop, calls=%fused_computation | loop fusion | flops 1572864 | bytes 4767744 | tf_op jit(solution)/shard_map/convert_element_type | solution.py:29
  52.9 5.3 %copy.32 = bf16[16,64,12,64]{3,0,2,1:T(8,128)(2,1)} copy(bf16[16,64,12,64]{3,2,1,0:T(8,128)(2,1)S(1)} %divide_convert_fusion) | data formatting | bytes 3145728 | tf_op jit(solution)/shard_map/convert_element_type | solution.py:29
  58.2 6.2 %reshape.33 = bf16[64,2,6144]{2,1,0:T(2,128)(2,1)} reshape(bf16[64,12,16,64]{3,2,1,0:T(8,128)(2,1)} %bitcast.18) | data formatting | bytes 3145728
  64.5 13.0 %all-to-all-start = ((bf16[64,2,6144]{2,1,0:T(2,128)(2,1)}), bf16[64,2,6144]{2,1,0:T(2,128)(2,1)}, u32[]{:S(2)}, u32[]{:S(2)}) async-start(bf16[64,2,6144]{2,1,0:T(2,128)(2,1)} %reshape.33), calls=%async_computation | async-start | bytes 3145728 | tf_op jit(solution)/shard_map/all_to_all | solution.py:37
  77.5 0.7 all-gather.3.cloned.1.call-update
  78.2 1.3 dynamic-slice
  80.2 0.2 dynamic-update-slice
  80.4 165.2 %all-reduce = bf16[384]{0:T(512)(128)(2,1)S(1)} all-reduce(bf16[384]{0:T(512)(128)(2,1)S(1)} %dynamic-update-slice), channel_id=1, replica_groups=mesh['cross'=16,'node'=64] {'node'}, use_global_device_ids=true, to_apply=%add | all-reduce | flops 384 | bytes 1536
  245.6 0.8 mul.28
  246.4 1.0 mul.29
  247.4 0.3 copy.28
  247.7 1.0 copy.29
  248.7 6.3 %reshape.34 = bf16[64,12,16,64]{3,2,1,0:T(8,128)(2,1)} reshape(bf16[64,2,6144]{2,1,0:T(2,128)(2,1)} %all-to-all-done) | data formatting | bytes 3145728
  255.1 3.9 %multiply_reduce_fusion = bf16[16,12,64]{2,0,1:T(8,128)(2,1)S(1)} fusion(f32[16,64,12]{0,2,1:T(8,128)} %copy.29, bf16[64,12,16,64]{3,2,1,0:T(8,128)(2,1)} %reshape.34), kind=kLoop, calls=%fused_computation.1 | loop fusion | flops 2347008 | bytes 1646592 | tf_op jit(solution)/shard_map/reduce_sum | solution.py:42
  259.0 0.7 reshape.35
  259.7 12.6 %all-to-all-start.2 = ((bf16[16,2,384]{2,1,0:T(2,128)(2,1)}), bf16[16,2,384]{2,1,0:T(2,128)(2,1)S(1)}, u32[]{:S(2)}, u32[]{:S(2)}) async-start(bf16[16,2,384]{2,1,0:T(2,128)(2,1)} %reshape.35), calls=%async_computation.2 | async-start | bytes 49152 | tf_op jit(solution)/shard_map/all_to_all | solution.py:43
  272.4 4.7 %copy.24 = f32[64,192,64]{1,0,2:T(8,128)} copy(bf16[64,192,64]{1,2,0:T(8,128)(2,1)} %all-gather.3.cloned.1.call-done) | data formatting | bytes 4718592 | tf_op jit(solution)/shard_map/convert_element_type | solution.py:17
  277.1 5.2 %reshape.32 = f32[12288,64]{0,1:T(8,128)} reshape(f32[64,192,64]{1,0,2:T(8,128)} %copy.24) | data formatting | bytes 6291456 | tf_op jit(solution)/shard_map/convert_element_type | solution.py:17
  282.4 3.7 %fusion.3 = bf16[128,64]{0,1:T(8,128)(2,1)} fusion(bf16[128,12288]{1,0:T(8,128)(2,1)S(1)} %copy-done, f32[12288,64]{0,1:T(8,128)} %reshape.32, f32[12288]{0:T(1024)S(1)} %mul.29), kind=kOutput, calls=%fused_computation.7 | convolution fusion | flops 202907648 | bytes 6356992 | tf_op jit(solution)/shard_map/dot_general | solution.py:20
  286.1 0.1 reshape.36
  286.2 0.6 convert_reduce_fusion
  (12 shorter events, 0.1 us)
Async XLA Ops:
  7.2 1.9 copy-start
  15.4 49.0 %all-to-all-start.1 = ((bf16[16,64,12]{2,0,1:T(8,128)(2,1)}), bf16[16,64,12]{2,0,1:T(8,128)(2,1)S(1)}, u32[]{:S(2)}, u32[]{:S(2)}) async-start(bf16[16,64,12]{2,0,1:T(8,128)(2,1)} %copy.27), calls=%async_computation.1 | async-start | bytes 524288 | tf_op jit(solution)/shard_map/all_to_all | solution.py:38
  58.2 21.9 %copy-start.1 = (f32[1,6]{1,0:T(1,128)S(1)}, f32[1,6]{1,0:T(1,128)}, u32[]{:S(2)}) copy-start(f32[1,6]{1,0:T(1,128)} %param.6) | copy-start | bytes 76
  64.5 184.3 %all-to-all-start = ((bf16[64,2,6144]{2,1,0:T(2,128)(2,1)}), bf16[64,2,6144]{2,1,0:T(2,128)(2,1)}, u32[]{:S(2)}, u32[]{:S(2)}) async-start(bf16[64,2,6144]{2,1,0:T(2,128)(2,1)} %reshape.33), calls=%async_computation | async-start | bytes 3145728 | tf_op jit(solution)/shard_map/all_to_all | solution.py:37
  77.5 194.9 %all-gather.3.cloned.1.call-start = ((), (), s32[]{:S(2)}) async-start(), calls=%async_computation.3 | async-start | bytes 2129920 | tf_op jit(solution)/shard_map/all_gather | solution.py:11
  259.7 26.3 %all-to-all-start.2 = ((bf16[16,2,384]{2,1,0:T(2,128)(2,1)}), bf16[16,2,384]{2,1,0:T(2,128)(2,1)S(1)}, u32[]{:S(2)}, u32[]{:S(2)}) async-start(bf16[16,2,384]{2,1,0:T(2,128)(2,1)} %reshape.35), calls=%async_computation.2 | async-start | bytes 49152 | tf_op jit(solution)/shard_map/all_to_all | solution.py:43
Sparse Core Ops, SparseCore 0:
  82.8 105.9 all-gather.2
where the time goes:
time: 296 us; the launch traced here: 294 us
  blocking collectives  165 us (56%)
  local copies, waits for them, and re-layouts  51.3 us (17%)
  starting transfers between devices  43.9 us (15%)
  between operations  14.8 us (5%)
  other arithmetic  11 us (4%)
  matrix products  6.67 us (2%)
    unnamed x1, blocking collectives  165 us
    all_to_all x1, starting transfers between devices, shards(): lax.all_to_all(scale3.astype(jnp.bfloat16), 'node', split_axis=1, concat_...  18.2 us
    unnamed x11, local copies, waits for them, and re-layouts  16.8 us
    all_to_all x1, starting transfers between devices, shards(): lax.all_to_all(packed4, 'node', split_axis=1, concat_axis=1, tiled=True)  13 us
    all_to_all x1, starting transfers between devices, shards(): lax.all_to_all(partial_sum.astype(jnp.bfloat16), 'cross', split_axis=0, c...  12.6 us
    convert_element_type x2, local copies, waits for them, and re-layouts, shards(): piece_codes.astype(jnp.float32)  9.97 us
    reshape x1, local copies, waits for them, and re-layouts, shards(): blocks = term.reshape(width // span, span * channels)  8.21 us
  transfers between devices with their start and end apart: 4, of which 0 were waited for; matrix products, arithmetic and copies ran while one was open for 20% of the time, Pallas kernels for 0%

commit v1 on v0

v1 whole, which is shorter than its diff:
```python
import jax
import jax.numpy as jnp
import numpy as np
from jax import lax
from jax.experimental import pallas as pl
from jax.experimental.pallas import tpu as pltpu
from jax.sharding import Mesh
from jax.sharding import PartitionSpec as P

AXES = ("z", "yl", "yh", "x", "c")
SIZES = (8, 2, 4, 8, 2)
D, HD, TOK = 12288, 64, 128
BF, F32 = jnp.bfloat16, jnp.float32
NT = (((1,), (1,)), ((), ()))
SPAN = 384


def groups():
    dev = np.arange(1024).reshape(8, 8, 8, 2)
    line = [dev[:, y, x, 0] for y in range(8) for x in range(8)] + [dev[z, :, x, 1] for z in range(8) for x in range(8)]
    plane = [dev[z, :, :, 0].reshape(-1) for z in range(8)] + [dev[:, y, :, 1].reshape(-1) for y in range(8)]
    return [g.tolist() for g in line], [g.tolist() for g in plane]


def scale_kernel(codes_ref, scale_ref, out_ref):
    lane = lax.broadcasted_iota(jnp.int32, (HD, 192), 1) // 32
    factor = jnp.full((HD, 192), scale_ref[0, 0], F32)
    for k in range(1, 6):
        factor = jnp.where(lane == k, scale_ref[0, k], factor)
    weights = (codes_ref[...].astype(F32) * factor).astype(BF)
    for k in range(8):
        out_ref[k] = weights


def pair_kernel(in_ref, out_ref):
    for k in range(4):
        out_ref[k, :, 0:192] = in_ref[2 * k]
        out_ref[k, :, 192:384] = in_ref[2 * k + 1]


def term_kernel(core_ref, tokens_ref, upstream_ref, out_ref):
    step = pl.program_id(0)
    core = core_ref[0]
    row = lax.broadcasted_iota(jnp.int32, (192, SPAN), 0)
    col = lax.broadcasted_iota(jnp.int32, (192, SPAN), 1)
    first = row + 12 * (row // 12)
    pick = jnp.concatenate([(col == first).astype(F32), (col == first + 12).astype(F32)], axis=1).astype(BF)
    blank = jnp.zeros((HD, SPAN), BF)
    for b in range(tokens_ref.shape[1] // SPAN):
        part = jnp.dot(upstream_ref[...], tokens_ref[:, SPAN * b : SPAN * (b + 1)], preferred_element_type=F32).astype(BF)
        both = jnp.concatenate(
            [jnp.concatenate([part, blank], axis=1), jnp.concatenate([blank, part], axis=1)], axis=0
        )
        rows = lax.dot_general(pick, both, NT, preferred_element_type=F32).astype(BF)
        for half in range(2):
            block = step * (tokens_ref.shape[1] // 192) + 2 * b + half
            z, y = block // 8, block % 8
            out_ref[jnp.where(core == 0, z * 8 + y, y * 8 + z)] = rows[96 * half : 96 * half + 96]


def sum_kernel(in_ref, out_ref, total_ref):
    total = in_ref[0].astype(F32)
    for k in range(1, 8):
        total += in_ref[k].astype(F32)
    total_ref[...] = total
    for k in range(out_ref.shape[0]):
        out_ref[k] = total_ref[12 * k : 12 * k + 12].astype(BF)


def values_kernel(weights_ref, tokens_ref, out_ref):
    total = jnp.zeros((HD, TOK), F32)
    for yh in range(4):
        for x in range(8):
            at = SPAN * (yh * 8 + x)
            total += lax.dot_general(
                weights_ref[x, yh], tokens_ref[:, at : at + SPAN], NT, preferred_element_type=F32
            )
    out_ref[...] = total.astype(BF)


def shards(tokens, codes, code_scale, upstream):
    line, plane = groups()
    core = lax.axis_index("c")
    vmem = pl.BlockSpec(memory_space=pltpu.VMEM)
    smem = pl.BlockSpec(memory_space=pltpu.SMEM)
    params = pltpu.CompilerParams(vmem_limit_bytes=40 * 2**20)

    copies = pl.pallas_call(
        scale_kernel,
        out_shape=jax.ShapeDtypeStruct((8, HD, 192), BF),
        in_specs=[vmem, smem],
        out_specs=vmem,
        name="scale",
    )(codes, code_scale)
    near = lax.all_to_all(copies, ("yh", "c"), split_axis=0, concat_axis=0, tiled=True)
    paired = pl.pallas_call(
        pair_kernel,
        out_shape=jax.ShapeDtypeStruct((4, HD, SPAN), BF),
        in_specs=[vmem],
        out_specs=vmem,
        name="pair",
    )(near)
    weights = lax.all_gather(paired, "x", axis=0, tiled=False)

    width = 3072
    term = pl.pallas_call(
        term_kernel,
        grid=(D // width,),
        out_shape=jax.ShapeDtypeStruct((64, 96, 128), BF),
        in_specs=[
            smem,
            pl.BlockSpec((TOK, width), lambda i: (0, i)),
            pl.BlockSpec((HD, TOK), lambda i: (0, 0)),
        ],
        out_specs=pl.BlockSpec((64, 96, 128), lambda i: (0, 0, 0)),
        compiler_params=params,
        cost_estimate=pl.CostEstimate(flops=2 * D * TOK * HD, bytes_accessed=5 * 2**20, transcendentals=0),
        name="term",
    )(core.reshape(1), tokens, upstream.T)
    arrived = lax.all_to_all(
        term.reshape(8, 768, 128), AXES, split_axis=0, concat_axis=0, axis_index_groups=line, tiled=True
    )
    partial_sum = pl.pallas_call(
        sum_kernel,
        grid=(4,),
        out_shape=jax.ShapeDtypeStruct((64, 12, 128), BF),
        in_specs=[pl.BlockSpec((8, 192, 128), lambda i: (0, i, 0))],
        out_specs=pl.BlockSpec((16, 12, 128), lambda i: (i, 0, 0)),
        scratch_shapes=[pltpu.VMEM((192, 128), F32)],
        compiler_params=params,
        cost_estimate=pl.CostEstimate(flops=2 * D * HD, bytes_accessed=2 * 2**20, transcendentals=0),
        name="sum",
    )(arrived)
    last = lax.all_to_all(partial_sum, AXES, split_axis=0, concat_axis=0, axis_index_groups=plane, tiled=True)
    chip = lax.psum(jnp.sum(last.astype(F32), axis=0), "c")
    weight_grad = jnp.where(core == 0, chip[:, :HD], chip[:, HD:])

    values = pl.pallas_call(
        values_kernel,
        out_shape=jax.ShapeDtypeStruct((HD, TOK), BF),
        in_specs=[vmem, vmem],
        out_specs=vmem,
        compiler_params=params,
        cost_estimate=pl.CostEstimate(flops=2 * D * TOK * HD, bytes_accessed=5 * 2**20, transcendentals=0),
        name="values",
    )(weights, tokens)
    return values.T, weight_grad


def solution(mesh):
    fine = Mesh(mesh.devices.reshape(SIZES), AXES)
    rows = P(AXES, None)
    columns = P(None, ("yh", "x", "c"))
    return jax.shard_map(
        shards, mesh=fine, in_specs=(rows, columns, columns, rows), out_specs=(rows, rows), check_vma=False
    )
```

time: 296 us -> 112 us (0.38)
  blocking collectives: 165 us -> 8.07 us
  local copies, waits for them, and re-layouts: 51.3 us -> 5.86 us
  waiting for transfers between devices: 0.71 us -> 31.1 us
  Pallas kernels: 0 us -> 14.5 us
  other arithmetic: 11 us -> 0.75 us
  matrix products: 6.67 us -> 0 us
  starting transfers between devices: 43.9 us -> 37.6 us
    unnamed x1 -> x0, blocking collectives: 165 us -> none
    all_to_all x3, waiting for transfers between devices: 0.01 us -> 20.1 us  [the longest x1 19.3 us: shards(): lax.all_to_all(term.reshape(8, 768, 128), AXES, split_axis=0, concat_axis...]
    convert_element_type x6 -> x0, local copies, waits for them, and re-layouts: 17.2 us -> none  [the longest x2 9.97 us: shards(): piece_codes.astype(jnp.float32)]
    pallas_call x0 -> x5, Pallas kernels: none -> 14.5 us  [the longest x1 5.68 us: shards(): pl.pallas_call(term_kernel, grid=(D // width,), out_shape=jax.ShapeDtypeS...]
    all_gather x1, waiting for transfers between devices: 0.02 us -> 11 us  [shards(): weights = lax.all_gather(paired, 'x', axis=0, tiled=False)]
    unnamed x11 -> x12, local copies, waits for them, and re-layouts: 16.8 us -> 5.86 us
    reshape x1 -> x0, local copies, waits for them, and re-layouts: 8.21 us -> none  [shards(): blocks = term.reshape(width // span, span * channels)]
    psum x0 -> x1, blocking collectives: none -> 8.07 us  [shards(): chip = lax.psum(jnp.sum(last.astype(F32), axis=0), 'c')]
  transfers between devices with their start and end apart: 4 -> 4, of which waited for: 0 -> 4; matrix products, arithmetic and copies ran while one was open for 20% -> 0% of each run, Pallas kernels for 0% -> 12%
where the time goes in v1:
time: 112 us
  starting transfers between devices  37.6 us (34%)
  waiting for transfers between devices  31.1 us (28%)
  Pallas kernels  14.5 us (13%)
  between operations  14.1 us (13%)
  blocking collectives  8.07 us (7%)
  local copies, waits for them, and re-layouts  5.86 us (5%)
    all_to_all x1, waiting for transfers between devices, shards(): lax.all_to_all(term.reshape(8, 768, 128), AXES, split_axis=0, concat_axis...  19.3 us
    all_to_all x1, starting transfers between devices, shards(): lax.all_to_all(copies, ('yh', 'c'), split_axis=0, concat_axis=0, tiled=True)  17.5 us
    all_to_all x1, starting transfers between devices, shards(): lax.all_to_all(partial_sum, AXES, split_axis=0, concat_axis=0, axis_index...  13.6 us
    all_gather x1, waiting for transfers between devices, shards(): weights = lax.all_gather(paired, 'x', axis=0, tiled=False)  11 us
    psum x1, blocking collectives, shards(): chip = lax.psum(jnp.sum(last.astype(F32), axis=0), 'c')  8.07 us
    all_to_all x1, starting transfers between devices, shards(): lax.all_to_all(term.reshape(8, 768, 128), AXES, split_axis=0, concat_axis...  6.46 us
    unnamed x12, local copies, waits for them, and re-layouts  5.86 us
    pallas_call x1, Pallas kernels, shards(): pl.pallas_call(term_kernel, grid=(D // width,), out_shape=jax.ShapeDtypeS...  5.68 us
  transfers between devices with their start and end apart: 4, of which 4 were waited for; matrix products, arithmetic and copies ran while one was open for 0% of the time, Pallas kernels for 12%

profile of v1, /device:TPU:1, one launch (start us, length us, event | category | flops | bytes accessed | tf_op | source)
XLA Modules:
  0.0 111.8 jit_solution(15285928626761138354)
XLA Ops:
  7.2 1.5 %scale.1 = bf16[8,64,192]{2,1,0:T(8,128)(2,1)} custom-call(bf16[64,192]{1,0:T(8,128)(2,1)} %codes_ref.1, f32[1,6]{1,0:T(1,128)} %scale_ref.1), custom_call_target="tpu_custom_call" | custom-call | tf_op jit(solution)/shard_map/scale/pallas_call | solution.py:88
  8.7 17.5 %all-to-all-start = ((bf16[8,64,192]{2,1,0:T(8,128)(2,1)}), bf16[8,64,192]{2,1,0:T(8,128)(2,1)S(1)}, u32[]{:S(2)}, u32[]{:S(2)}) async-start(bf16[8,64,192]{2,1,0:T(8,128)(2,1)} %scale.1), calls=%async_computation | async-start | bytes 524288 | tf_op jit(solution)/shard_map/all_to_all | solution.py:95
  26.1 0.0 copy-start
  26.1 1.9 %copy-done = bf16[128,12288]{1,0:T(8,128)(2,1)S(1)} copy-done((bf16[128,12288]{1,0:T(8,128)(2,1)S(1)}, bf16[128,12288]{1,0:T(8,128)(2,1)}, u32[]{:S(2)}) %copy-start) | copy-done | bytes 3145752
  28.0 0.0 copy-start.4
  28.0 0.7 copy-done.4
  28.8 5.7 %term.1 = bf16[64,96,128]{2,1,0:T(8,128)(2,1)S(1)} custom-call(s32[1]{0:T(128)} %bitcast.2.core_ref, bf16[128,12288]{1,0:T(8,128)(2,1)S(1)} %copy-done, bf16[64,128]{1,0:T(8,128)(2,1)S(1)} %bitcast.7), custom_call_target="tpu_custom_call" | custom-call | flops 201326592 | bytes 5242880 | tf_op jit(solution)/shard_map/term/pallas_call | solution.py:106
  34.4 0.0 copy-start.2
  34.5 1.1 %copy-done.2 = bf16[64,96,128]{2,1,0:T(8,128)(2,1)} copy-done((bf16[64,96,128]{2,1,0:T(8,128)(2,1)}, bf16[64,96,128]{2,1,0:T(8,128)(2,1)S(1)}, u32[]{:S(2)}) %copy-start.2) | copy-done | bytes 1572888
  35.6 0.3 all-to-all-done.in_ref
  35.8 0.0 copy-start.5
  35.8 0.0 copy-start.1
  35.8 0.7 copy-done.5
  36.5 6.5 %all-to-all-start.1 = ((bf16[8,768,128]{2,1,0:T(8,128)(2,1)}), bf16[8,768,128]{2,1,0:T(8,128)(2,1)}, u32[]{:S(2)}, u32[]{:S(2)}) async-start(bf16[8,768,128]{2,1,0:T(8,128)(2,1)} %bitcast.5), calls=%async_computation.1 | async-start | bytes 3145728 | tf_op jit(solution)/shard_map/all_to_all | solution.py:120
  43.0 0.0 all-gather.3.cloned.1.call-start
  43.1 1.7 %pair.1 = bf16[4,64,384]{2,1,0:T(8,128)(2,1)} custom-call(bf16[8,64,192]{2,1,0:T(8,128)(2,1)} %copy-done.5), custom_call_target="tpu_custom_call" | custom-call | tf_op jit(solution)/shard_map/pair/pallas_call | solution.py:96
  44.8 0.0 all-gather.3.cloned.1.call-update
  44.8 19.3 %all-to-all-done.1.in_ref = bf16[8,768,128]{2,1,0:T(8,128)(2,1)} async-done(((bf16[8,768,128]{2,1,0:T(8,128)(2,1)}), bf16[8,768,128]{2,1,0:T(8,128)(2,1)}, u32[]{:S(2)}, u32[]{:S(2)}) %all-to-all-start.1) | async-done | bytes 1572896 | tf_op jit(solution)/shard_map/all_to_all | solution.py:120
  64.1 3.4 %sum.1 = bf16[64,12,128]{2,1,0:T(8,128)(2,1)} custom-call(bf16[8,768,128]{2,1,0:T(8,128)(2,1)} %all-to-all-done.1.in_ref), custom_call_target="tpu_custom_call" | custom-call | flops 1572864 | bytes 2097152 | tf_op jit(solution)/shard_map/sum/pallas_call | solution.py:123
  67.5 13.6 %all-to-all-start.2 = ((bf16[64,12,128]{2,1,0:T(8,128)(2,1)}), bf16[64,12,128]{2,1,0:T(8,128)(2,1)S(1)}, u32[]{:S(2)}, u32[]{:S(2)}) async-start(bf16[64,12,128]{2,1,0:T(8,128)(2,1)} %sum.1), calls=%async_computation.2 | async-start | bytes 524288 | tf_op jit(solution)/shard_map/all_to_all | solution.py:134
  81.1 11.0 %all-gather.3.cloned.1.call-done = bf16[32,64,384]{2,1,0:T(8,128)(2,1)} async-done(((bf16[4,64,384]{2,1,0:T(8,128)(2,1)}), bf16[32,64,384]{2,1,0:T(8,128)(2,1)}) %all-gather.3.cloned.1.call-update) | async-done | bytes 1572880 | tf_op jit(solution)/shard_map/all_gather | solution.py:103
  92.1 0.0 copy-done.1
  92.1 0.0 copy-start.3
  92.1 1.4 %copy-done.3 = bf16[32,64,384]{2,1,0:T(8,128)(2,1)S(1)} copy-done((bf16[32,64,384]{2,1,0:T(8,128)(2,1)S(1)}, bf16[32,64,384]{2,1,0:T(8,128)(2,1)}, u32[]{:S(2)}) %copy-start.3) | copy-done | bytes 1572888
  93.5 2.1 %values.1 = bf16[64,128]{1,0:T(8,128)(2,1)} custom-call(bf16[8,4,64,384]{3,2,1,0:T(8,128)(2,1)S(1)} %bitcast.6, bf16[128,12288]{1,0:T(8,128)(2,1)S(1)} %copy-done.1), custom_call_target="tpu_custom_call" | custom-call | flops 201326592 | bytes 5242880 | tf_op jit(solution)/shard_map/values/pallas_call | solution.py:138
  95.6 0.5 all-to-all-done.2
  96.2 0.1 convert_reduce_fusion
  96.3 8.1 %psum.7 = f32[12,128]{1,0:T(8,128)S(1)} all-reduce(f32[12,128]{1,0:T(8,128)S(1)} %convert_reduce_fusion), channel_id=1, replica_groups=mesh['z'=8,'yl'=2,'yh'=4,'x'=8,'c'=2] {'c'}, use_global_device_ids=true, to_apply=%region_1.0 | all-reduce | flops 1536 | bytes 12288 | tf_op jit(solution)/shard_map/psum | solution.py:135
  104.3 0.7 slice_select_fusion
Async XLA Ops:
  8.7 27.2 %all-to-all-start = ((bf16[8,64,192]{2,1,0:T(8,128)(2,1)}), bf16[8,64,192]{2,1,0:T(8,128)(2,1)S(1)}, u32[]{:S(2)}, u32[]{:S(2)}) async-start(bf16[8,64,192]{2,1,0:T(8,128)(2,1)} %scale.1), calls=%async_computation | async-start | bytes 524288 | tf_op jit(solution)/shard_map/all_to_all | solution.py:95
  26.1 1.9 %copy-start = (bf16[128,12288]{1,0:T(8,128)(2,1)S(1)}, bf16[128,12288]{1,0:T(8,128)(2,1)}, u32[]{:S(2)}) copy-start(bf16[128,12288]{1,0:T(8,128)(2,1)} %tokens_ref.3) | copy-start | bytes 9437188
  28.0 0.7 copy-start.4
  34.4 1.1 %copy-start.2 = (bf16[64,96,128]{2,1,0:T(8,128)(2,1)}, bf16[64,96,128]{2,1,0:T(8,128)(2,1)S(1)}, u32[]{:S(2)}) copy-start(bf16[64,96,128]{2,1,0:T(8,128)(2,1)S(1)} %term.1) | copy-start | bytes 4718596
  35.8 0.7 copy-start.5
  35.8 56.2 %copy-start.1 = (bf16[128,12288]{1,0:T(8,128)(2,1)S(1)}, bf16[128,12288]{1,0:T(8,128)(2,1)}, u32[]{:S(2)}) copy-start(bf16[128,12288]{1,0:T(8,128)(2,1)} %tokens_ref.3) | copy-start | bytes 9437188
  36.5 27.5 %all-to-all-start.1 = ((bf16[8,768,128]{2,1,0:T(8,128)(2,1)}), bf16[8,768,128]{2,1,0:T(8,128)(2,1)}, u32[]{:S(2)}, u32[]{:S(2)}) async-start(bf16[8,768,128]{2,1,0:T(8,128)(2,1)} %bitcast.5), calls=%async_computation.1 | async-start | bytes 3145728 | tf_op jit(solution)/shard_map/all_to_all | solution.py:120
  43.0 49.1 %all-gather.3.cloned.1.call-start = ((), (), s32[]{:S(2)}) async-start(), calls=%async_computation.3 | async-start | bytes 1769472 | tf_op jit(solution)/shard_map/all_gather | solution.py:103
  67.5 28.7 %all-to-all-start.2 = ((bf16[64,12,128]{2,1,0:T(8,128)(2,1)}), bf16[64,12,128]{2,1,0:T(8,128)(2,1)S(1)}, u32[]{:S(2)}, u32[]{:S(2)}) async-start(bf16[64,12,128]{2,1,0:T(8,128)(2,1)} %sum.1), calls=%async_computation.2 | async-start | bytes 524288 | tf_op jit(solution)/shard_map/all_to_all | solution.py:134
  92.1 1.4 %copy-start.3 = (bf16[32,64,384]{2,1,0:T(8,128)(2,1)S(1)}, bf16[32,64,384]{2,1,0:T(8,128)(2,1)}, u32[]{:S(2)}) copy-start(bf16[32,64,384]{2,1,0:T(8,128)(2,1)} %all-gather.3.cloned.1.call-done) | copy-start | bytes 4718596
Sparse Core Ops, SparseCore 0:
  46.5 45.5 all-gather.2

commit v2 on v0

v2 whole, which is shorter than its diff:
```python
import jax
import jax.numpy as jnp
import numpy as np
from jax import lax
from jax.experimental import pallas as pl
from jax.experimental.pallas import tpu as pltpu
from jax.sharding import Mesh
from jax.sharding import PartitionSpec as P

AXES = ("z", "yl", "yh", "x", "c")
SIZES = (8, 2, 4, 8, 2)
D, HD, TOK = 12288, 64, 128
BF, F32 = jnp.bfloat16, jnp.float32
NT = (((1,), (1,)), ((), ()))
SPAN = 384


def groups():
    dev = np.arange(1024).reshape(SIZES)
    whole = dev.transpose(0, 2, 1, 3, 4).reshape(8, 8, 8, 2)
    near = [
        np.array([[dev[pz + 2 * (t ^ (yh // 2 * 2 + x // 2)), yl, yh, 2 * x + px, c] for x in range(4)] for yh in range(4)]).reshape(-1)
        for t in range(4)
        for pz, yl, px, c in np.ndindex(2, 2, 2, 2)
    ]
    rest = [dev[pz::2, yl, :, px::2, c].reshape(-1) for c in range(2) for pz in range(2) for yl in range(2) for px in range(2)]
    cube = []
    for core in range(2):
        for base in np.ndindex(4, 4, 4):
            corner = [2 * i + core for i in base]
            members = {}
            for step in np.ndindex(2, 2, 2):
                z, y, x = [(i + j) % 8 for i, j in zip(corner, step)]
                members[z % 2 * 4 + y % 2 * 2 + x % 2] = whole[z, y, x, core]
            cube.append(np.array([members[k] for k in range(8)]))
    return [[g.tolist() for g in kind] for kind in (near, cube, rest)]


def scale_kernel(at_ref, codes_ref, scale_ref, out_ref):
    lane = lax.broadcasted_iota(jnp.int32, (16, 192), 1) // 32
    factor = jnp.full((16, 192), scale_ref[0, 0], F32)
    for k in range(1, 6):
        factor = jnp.where(lane == k, scale_ref[0, k], factor)
    rows = codes_ref[pl.ds(pl.multiple_of(at_ref[0], 16), 16), :]
    weights = (rows.astype(F32) * factor).astype(BF)
    for k in range(16):
        out_ref[k] = weights


def term_kernel(core_ref, tokens_hbm, upstream_ref, own_hbm, send_hbm, tokens_ref, part_ref, out_ref, in_sem, out_sem):
    core = core_ref[0]
    reads = [
        pltpu.make_async_copy(tokens_hbm.at[:, 1536 * z : 1536 * (z + 1)], tokens_ref.at[z], in_sem.at[z])
        for z in range(8)
    ]
    for read in reads:
        read.start()
    source = lax.broadcasted_iota(jnp.int32, (768, 768), 0)
    place = lax.broadcasted_iota(jnp.int32, (768, 768), 1)
    line = source // 12
    target = 12 * (32 * (line % 2) + 16 * (line // 2 % 2) + line // 4) + source % 12
    move = (place == target).astype(F32).astype(BF)
    writes = []
    for half in range(2):
        for z in range(4):
            reads[4 * half + z].wait()
            part = jnp.dot(upstream_ref[...], tokens_ref[4 * half + z], preferred_element_type=F32).astype(BF)
            for yl in range(2):
                part_ref[HD * (2 * z + yl) : HD * (2 * z + yl + 1)] = part[:, 768 * yl : 768 * (yl + 1)]
        for owner in range(2):
            moved = jnp.dot(
                part_ref[...], move[:, SPAN * owner : SPAN * (owner + 1)], preferred_element_type=F32
            ).astype(BF)
            for z in range(4):
                for yl in range(2):
                    for px in range(2):
                        k = z % 2 * 4 + yl * 2 + px
                        at = SPAN * half + 192 * (z // 2)
                        out_ref[owner, k, :, at : at + 192] = moved[
                            HD * (2 * z + yl) : HD * (2 * z + yl + 1), 192 * px : 192 * (px + 1)
                        ]
        at = pl.ds(SPAN * half, SPAN)
        for i, (owner, out_hbm) in enumerate(((1 - core, send_hbm), (core, own_hbm))):
            writes.append(
                pltpu.make_async_copy(out_ref.at[owner, :, :, at], out_hbm.at[:, :, at], out_sem.at[2 * half + i])
            )
            writes[-1].start()
    for write in writes:
        write.wait()


def fill_kernel(near_ref, own_ref, other_ref, out_ref):
    out_ref[:, :, :768] = (own_ref[...].astype(F32) + other_ref[...].astype(F32)).astype(BF)
    for p in range(out_ref.shape[0]):
        for k in range(16):
            out_ref[p, 16 * (k // 4) : 16 * (k // 4 + 1), 768 + 192 * (k % 4) : 960 + 192 * (k % 4)] = near_ref[k]


def sum_kernel(in_ref, in_hbm, out_ref, weights_hbm, sem):
    step = pl.program_id(0)
    copy = pltpu.make_async_copy(in_hbm.at[:, :, pl.ds(768, 768)], weights_hbm, sem)

    @pl.when(step == 0)
    def _():
        copy.start()

    row = lax.broadcasted_iota(jnp.int32, (256, SPAN), 0)
    col = lax.broadcasted_iota(jnp.int32, (256, SPAN), 1)
    first = jnp.where(row % 8 < 6, 12 * (row // 8) + row % 8, -SPAN)
    pick = jnp.concatenate([(col == first).astype(F32), (col == first + 6).astype(F32)], axis=1).astype(BF)
    total = in_ref[0].astype(F32)
    for k in range(1, 8):
        total += in_ref[k].astype(F32)
    total = total.astype(BF)
    blank = jnp.zeros((HD, SPAN), BF)
    both = jnp.concatenate(
        [jnp.concatenate([total, blank], axis=1), jnp.concatenate([blank, total], axis=1)], axis=0
    )
    rows = lax.dot_general(pick, both, NT, preferred_element_type=F32)
    out_ref[...] = rows.reshape(32, 8, 128).astype(BF)

    @pl.when(step == 1)
    def _():
        copy.wait()


def values_kernel(core_ref, own_ref, other_ref, tokens_ref, out_ref):
    def product(first_ref, second_ref):
        total = jnp.zeros((HD, TOK), F32)
        for yh in range(4):
            for x in range(8):
                at = SPAN * (yh * 8 + x)
                halves = [
                    jnp.concatenate(
                        [
                            ref[2 * q + x % 2, 16 * yh : 16 * (yh + 1), 192 * (x // 2) : 192 * (x // 2 + 1)]
                            for q in range(4)
                        ],
                        axis=0,
                    )
                    for ref in (first_ref, second_ref)
                ]
                total += lax.dot_general(
                    jnp.concatenate(halves, axis=1), tokens_ref[:, at : at + SPAN], NT, preferred_element_type=F32
                )
        out_ref[...] = total.astype(BF)

    @pl.when(core_ref[0] == 0)
    def _():
        product(own_ref, other_ref)

    @pl.when(core_ref[0] != 0)
    def _():
        product(other_ref, own_ref)


def final_kernel(in_ref, out_ref):
    total = in_ref[0].astype(F32)
    for k in range(1, 64):
        total += in_ref[k].astype(F32)
    out_ref[0:6] = total[0:6, :HD]
    out_ref[6:12] = total[0:6, HD:]


def shards(tokens, codes, code_scale, upstream):
    near_groups, cube, rest = groups()
    core = lax.axis_index("c").reshape(1)
    vmem = pl.BlockSpec(memory_space=pltpu.VMEM)
    smem = pl.BlockSpec(memory_space=pltpu.SMEM)
    hbm = pl.BlockSpec(memory_space=pl.ANY)

    def exchange(value, who):
        return lax.all_to_all(value, AXES, split_axis=0, concat_axis=0, axis_index_groups=who, tiled=True)

    def swap(value):
        return lax.ppermute(value, "c", [(0, 1), (1, 0)])

    at = 16 * (2 * (lax.axis_index("z") % 2) + lax.axis_index("yl"))
    near = exchange(
        pl.pallas_call(
            scale_kernel,
            out_shape=jax.ShapeDtypeStruct((16, 16, 192), BF),
            in_specs=[smem, vmem, smem],
            out_specs=vmem,
            name="scale",
        )(at.reshape(1), codes, code_scale),
        near_groups,
    )
    own, send = pl.pallas_call(
        term_kernel,
        out_shape=[jax.ShapeDtypeStruct((8, HD, 768), BF)] * 2,
        in_specs=[smem, hbm, vmem],
        out_specs=[hbm, hbm],
        scratch_shapes=[
            pltpu.VMEM((8, TOK, 1536), BF),
            pltpu.VMEM((8 * HD, 768), BF),
            pltpu.VMEM((2, 8, HD, 768), BF),
            pltpu.SemaphoreType.DMA((8,)),
            pltpu.SemaphoreType.DMA((4,)),
        ],
        compiler_params=pltpu.CompilerParams(vmem_limit_bytes=60 * 2**20),
        cost_estimate=pl.CostEstimate(flops=2 * D * TOK * HD, bytes_accessed=5 * 2**20, transcendentals=0),
        name="term",
    )(core, tokens, upstream.T)
    send, near = lax.optimization_barrier((send, near))
    part = pl.BlockSpec((4, HD, 768), lambda i: (i, 0, 0))
    outgoing = pl.pallas_call(
        fill_kernel,
        grid=(2,),
        out_shape=jax.ShapeDtypeStruct((8, HD, 1536), BF),
        in_specs=[pl.BlockSpec((16, 16, 192), lambda i: (0, 0, 0)), part, part],
        out_specs=pl.BlockSpec((4, HD, 1536), lambda i: (i, 0, 0)),
        compiler_params=pltpu.CompilerParams(vmem_limit_bytes=40 * 2**20),
        name="fill",
    )(near, own, swap(send))
    arrived = exchange(outgoing, cube)
    partial_sum, weights = pl.pallas_call(
        sum_kernel,
        grid=(2,),
        out_shape=(jax.ShapeDtypeStruct((64, 8, 128), BF), jax.ShapeDtypeStruct((8, HD, 768), BF)),
        in_specs=[pl.BlockSpec((8, HD, SPAN), lambda i: (0, 0, i)), hbm],
        out_specs=(pl.BlockSpec((32, 8, 128), lambda i: (i, 0, 0)), hbm),
        scratch_shapes=[pltpu.SemaphoreType.DMA],
        compiler_params=pltpu.CompilerParams(vmem_limit_bytes=40 * 2**20),
        cost_estimate=pl.CostEstimate(flops=2 * D * HD, bytes_accessed=2 * 2**20, transcendentals=0),
        name="sum",
    )(arrived, arrived)
    last = exchange(partial_sum, rest)
    values = pl.pallas_call(
        values_kernel,
        out_shape=jax.ShapeDtypeStruct((HD, TOK), BF),
        in_specs=[smem, vmem, vmem, vmem],
        out_specs=vmem,
        compiler_params=pltpu.CompilerParams(vmem_limit_bytes=40 * 2**20),
        cost_estimate=pl.CostEstimate(flops=2 * D * TOK * HD, bytes_accessed=5 * 2**20, transcendentals=0),
        name="values",
    )(core, weights, swap(weights), tokens)
    last, values = lax.optimization_barrier((last, values))
    weight_grad = pl.pallas_call(
        final_kernel,
        out_shape=jax.ShapeDtypeStruct((12, HD), F32),
        in_specs=[vmem],
        out_specs=vmem,
        compiler_params=pltpu.CompilerParams(vmem_limit_bytes=4 * 2**20),
        name="final",
    )(last)
    return values.T, weight_grad


def solution(mesh):
    fine = Mesh(mesh.devices.reshape(SIZES), AXES)
    rows = P(AXES, None)
    columns = P(None, ("yh", "x", "c"))
    return jax.shard_map(
        shards, mesh=fine, in_specs=(rows, columns, columns, rows), out_specs=(rows, rows), check_vma=False
    )
```

time: 296 us -> 102 us (0.34)
  blocking collectives: 165 us -> 19.3 us
  local copies, waits for them, and re-layouts: 51.3 us -> 1.14 us
  waiting for transfers between devices: 0.71 us -> 22.1 us
  Pallas kernels: 0 us -> 14.3 us
  between operations: 14.8 us -> 0.72 us
  other arithmetic: 11 us -> 0 us
  matrix products: 6.67 us -> 0 us
    unnamed x1 -> x0, blocking collectives: 165 us -> none
    all_to_all x3 -> x2, waiting for transfers between devices: 0.01 us -> 20 us  [exchange(): lax.all_to_all(value, AXES, split_axis=0, concat_axis=0, axis_index_group...]
    all_to_all x0 -> x1, blocking collectives: none -> 19.3 us  [exchange(): lax.all_to_all(value, AXES, split_axis=0, concat_axis=0, axis_index_group...]
    convert_element_type x6 -> x0, local copies, waits for them, and re-layouts: 17.2 us -> none  [the longest x2 9.97 us: shards(): piece_codes.astype(jnp.float32)]
    unnamed x11 -> x4, local copies, waits for them, and re-layouts: 16.8 us -> 1.14 us
    pallas_call x0 -> x6, Pallas kernels: none -> 14.3 us  [the longest x1 6.43 us: shards(): pl.pallas_call(term_kernel, out_shape=[jax.ShapeDtypeStruct((8, HD, 768),...]
    reshape x1 -> x0, local copies, waits for them, and re-layouts: 8.21 us -> none  [shards(): blocks = term.reshape(width // span, span * channels)]
    dot_general x2 -> x0, matrix products: 6.67 us -> none  [the longest x1 3.69 us: shards(): lax.dot_general(tokens, weights, (((1,), (1,)), ((), ())), preferred_elem...]
  transfers between devices with their start and end apart: 4 -> 4, of which waited for: 0 -> 3; matrix products, arithmetic and copies ran while one was open for 20% -> 0% of each run, Pallas kernels for 0% -> 10%
where the time goes in v2:
time: 102 us; the launch traced here: 101 us
  starting transfers between devices  43.3 us (42%)
  waiting for transfers between devices  22.1 us (22%)
  blocking collectives  19.3 us (19%)
  Pallas kernels  14.3 us (14%)
  local copies, waits for them, and re-layouts  1.14 us (1%)
    all_to_all x2, starting transfers between devices, exchange(): lax.all_to_all(value, AXES, split_axis=0, concat_axis=0, axis_index_group...  37.3 us
    all_to_all x2, waiting for transfers between devices, exchange(): lax.all_to_all(value, AXES, split_axis=0, concat_axis=0, axis_index_group...  20 us
    all_to_all x1, blocking collectives, exchange(): lax.all_to_all(value, AXES, split_axis=0, concat_axis=0, axis_index_group...  19.3 us
    pallas_call x1, Pallas kernels, shards(): pl.pallas_call(term_kernel, out_shape=[jax.ShapeDtypeStruct((8, HD, 768),...  6.43 us
    ppermute x2, starting transfers between devices, swap(): return lax.ppermute(value, 'c', [(0, 1), (1, 0)])  6 us
    pallas_call x1, Pallas kernels, shards(): pl.pallas_call(values_kernel, out_shape=jax.ShapeDtypeStruct((HD, TOK), B...  3.59 us
    ppermute x2, waiting for transfers between devices, swap(): return lax.ppermute(value, 'c', [(0, 1), (1, 0)])  2.1 us
  transfers between devices with their start and end apart: 4, of which 3 were waited for; matrix products, arithmetic and copies ran while one was open for 0% of the time, Pallas kernels for 10%

profile of v2, /device:TPU:1, one launch (start us, length us, event | category | flops | bytes accessed | tf_op | source)
XLA Modules:
  0.0 100.8 jit_solution(14605577907677711515)
XLA Ops:
  0.6 1.5 %scale.1 = bf16[16,16,192]{2,1,0:T(8,128)(2,1)} custom-call(s32[1]{0:T(128)} %bitcast.2.at_ref, bf16[64,192]{1,0:T(8,128)(2,1)} %codes_ref.1, f32[1,6]{1,0:T(1,128)} %scale_ref.1), custom_call_target="tpu_custom_call" | custom-call | tf_op jit(solution)/shard_map/scale/pallas_call | solution.py:180
  2.1 27.1 %all-to-all-start = ((bf16[16,16,192]{2,1,0:T(8,128)(2,1)}), bf16[16,16,192]{2,1,0:T(8,128)(2,1)S(1)}, u32[]{:S(2)}, u32[]{:S(2)}) async-start(bf16[16,16,192]{2,1,0:T(8,128)(2,1)} %scale.1), calls=%async_computation | async-start | bytes 262144 | tf_op jit(solution)/shard_map/all_to_all | solution.py:173
  29.2 6.4 %term.1 = (bf16[8,64,768]{2,1,0:T(8,128)(2,1)}, bf16[8,64,768]{2,1,0:T(8,128)(2,1)}) custom-call(s32[1]{0:T(128)} %bitcast.core_ref, bf16[128,12288]{1,0:T(8,128)(2,1)} %tokens_ref.1, bf16[64,128]{1,0:T(8,128)(2,1)} %bitcast.4), custom_call_target="tpu_custom_call" | custom-call | flops 201326592 | bytes 5242880 | tf_op jit(solution)/shard_map/term/pallas_call | solution.py:189
  35.6 7.9 %all-to-all-done.near_ref = bf16[16,16,192]{2,1,0:T(8,128)(2,1)S(1)} async-done(((bf16[16,16,192]{2,1,0:T(8,128)(2,1)}), bf16[16,16,192]{2,1,0:T(8,128)(2,1)S(1)}, u32[]{:S(2)}, u32[]{:S(2)}) %all-to-all-start) | async-done | bytes 98336 | tf_op jit(solution)/shard_map/all_to_all | solution.py:173
  43.5 4.1 %collective-permute-start = (bf16[8,64,768]{2,1,0:T(8,128)(2,1)}, bf16[8,64,768]{2,1,0:T(8,128)(2,1)S(1)}, u32[]{:S(2)}, u32[]{:S(2)}) collective-permute-start(bf16[8,64,768]{2,1,0:T(8,128)(2,1)} %get-tuple-element.13), channel_id=1, source_target_pairs={{0,1},{1,0},{2,3},{3,2},{4,5},{5,4},{6,7},{7,6},{8,9},{9,8},{10,11... | collective-permute-start | bytes 2359304 | tf_op jit(solution)/shard_map/ppermute | solution.py:176
  47.6 2.1 %collective-permute-done.other_ref = bf16[8,64,768]{2,1,0:T(8,128)(2,1)S(1)} collective-permute-done((bf16[8,64,768]{2,1,0:T(8,128)(2,1)}, bf16[8,64,768]{2,1,0:T(8,128)(2,1)S(1)}, u32[]{:S(2)}, u32[]{:S(2)}) %collective-permute-start) | collective-permute-done | bytes 786464 | tf_op jit(solution)/shard_map/ppermute | solution.py:176
  49.7 0.0 copy-start.1
  49.7 1.1 %copy-done.1 = bf16[8,64,768]{2,1,0:T(8,128)(2,1)S(1)} copy-done((bf16[8,64,768]{2,1,0:T(8,128)(2,1)S(1)}, bf16[8,64,768]{2,1,0:T(8,128)(2,1)}, u32[]{:S(2)}) %copy-start.1) | copy-done | bytes 786456
  50.8 0.5 fill.1
  51.3 19.3 %all_to_all.15.in_ref.in_hbm = bf16[8,64,1536]{2,1,0:T(8,128)(2,1)S(1)} all-to-all(bf16[8,64,1536]{2,1,0:T(8,128)(2,1)S(1)} %fill.1), channel_id=1, replica_groups={{0,2,64,66,128,130,192,194},{4,6,68,70,132,134,196,198},{8,10,72,74,136..., dimensions={0} | all-to-all | bytes 3145728 | tf_op jit(solution)/shard_map/all_to_all | solution.py:173
  70.6 0.0 copy-start
  70.6 1.6 %sum.1 = (bf16[64,8,128]{2,1,0:T(8,128)(2,1)}, bf16[8,64,768]{2,1,0:T(8,128)(2,1)}) custom-call(bf16[8,64,1536]{2,1,0:T(8,128)(2,1)S(1)} %all_to_all.15.in_ref.in_hbm, bf16[8,64,1536]{2,1,0:T(8,128)(2,1)S(1)} %all_to_all.15.in_ref.in_hbm), custom_call_target="tpu_custom_call" | custom-call | flops 1572864 | bytes 2097152 | tf_op jit(solution)/shard_map/sum/pallas_call | solution.py:217
  72.2 1.9 %collective-permute-start.1 = (bf16[8,64,768]{2,1,0:T(8,128)(2,1)}, bf16[8,64,768]{2,1,0:T(8,128)(2,1)}, u32[]{:S(2)}, u32[]{:S(2)}) collective-permute-start(bf16[8,64,768]{2,1,0:T(8,128)(2,1)} %get-tuple-element.15.own_ref), channel_id=1, source_target_pairs={{0,1},{1,0},{2,3},{3,2},{4,5},{5,4},{6,7},{7,6},{8,9},{9,8},{10,11... | collective-permute-start | bytes 2359304 | tf_op jit(solution)/shard_map/ppermute | solution.py:176
  74.1 10.2 %all-to-all-start.2 = ((bf16[64,8,128]{2,1,0:T(8,128)(2,1)}), bf16[64,8,128]{2,1,0:T(8,128)(2,1)S(1)}, u32[]{:S(2)}, u32[]{:S(2)}) async-start(bf16[64,8,128]{2,1,0:T(8,128)(2,1)} %get-tuple-element.14), calls=%async_computation.2 | async-start | bytes 262144 | tf_op jit(solution)/shard_map/all_to_all | solution.py:173
  84.4 0.0 collective-permute-done.1.other_ref
  84.4 0.0 copy-done
  84.4 3.6 %values.1 = bf16[64,128]{1,0:T(8,128)(2,1)} custom-call(s32[1]{0:T(128)} %bitcast.core_ref, bf16[8,64,768]{2,1,0:T(8,128)(2,1)} %get-tuple-element.15.own_ref, bf16[8,64,768]{2,1,0:T(8,128)(2,1)} %collective-permute-done.1.other_ref, bf16[128,12288]{1,0:T(8,128)(2,1)S(1)} %copy-done), custom_call_target="tpu_custom_call" | custom-call | flops 201326592 | bytes 5242880 | tf_op jit(solution)/shard_map/values/pallas_call | solution.py:229
  88.0 12.1 %all-to-all-done.2.in_ref = bf16[64,8,128]{2,1,0:T(8,128)(2,1)S(1)} async-done(((bf16[64,8,128]{2,1,0:T(8,128)(2,1)}), bf16[64,8,128]{2,1,0:T(8,128)(2,1)S(1)}, u32[]{:S(2)}, u32[]{:S(2)}) %all-to-all-start.2) | async-done | bytes 131104 | tf_op jit(solution)/shard_map/all_to_all | solution.py:173
  100.1 0.7 final.1
Async XLA Ops:
  2.1 41.4 %all-to-all-start = ((bf16[16,16,192]{2,1,0:T(8,128)(2,1)}), bf16[16,16,192]{2,1,0:T(8,128)(2,1)S(1)}, u32[]{:S(2)}, u32[]{:S(2)}) async-start(bf16[16,16,192]{2,1,0:T(8,128)(2,1)} %scale.1), calls=%async_computation | async-start | bytes 262144 | tf_op jit(solution)/shard_map/all_to_all | solution.py:173
  43.5 6.2 %collective-permute-start = (bf16[8,64,768]{2,1,0:T(8,128)(2,1)}, bf16[8,64,768]{2,1,0:T(8,128)(2,1)S(1)}, u32[]{:S(2)}, u32[]{:S(2)}) collective-permute-start(bf16[8,64,768]{2,1,0:T(8,128)(2,1)} %get-tuple-element.13), channel_id=1, source_target_pairs={{0,1},{1,0},{2,3},{3,2},{4,5},{5,4},{6,7},{7,6},{8,9},{9,8},{10,11... | collective-permute-start | bytes 2359304 | tf_op jit(solution)/shard_map/ppermute | solution.py:176
  49.7 1.1 %copy-start.1 = (bf16[8,64,768]{2,1,0:T(8,128)(2,1)S(1)}, bf16[8,64,768]{2,1,0:T(8,128)(2,1)}, u32[]{:S(2)}) copy-start(bf16[8,64,768]{2,1,0:T(8,128)(2,1)} %get-tuple-element.12.own_ref) | copy-start | bytes 2359300
  70.6 13.8 %copy-start = (bf16[128,12288]{1,0:T(8,128)(2,1)S(1)}, bf16[128,12288]{1,0:T(8,128)(2,1)}, u32[]{:S(2)}) copy-start(bf16[128,12288]{1,0:T(8,128)(2,1)} %tokens_ref.1) | copy-start | bytes 9437188
  72.2 12.2 %collective-permute-start.1 = (bf16[8,64,768]{2,1,0:T(8,128)(2,1)}, bf16[8,64,768]{2,1,0:T(8,128)(2,1)}, u32[]{:S(2)}, u32[]{:S(2)}) collective-permute-start(bf16[8,64,768]{2,1,0:T(8,128)(2,1)} %get-tuple-element.15.own_ref), channel_id=1, source_target_pairs={{0,1},{1,0},{2,3},{3,2},{4,5},{5,4},{6,7},{7,6},{8,9},{9,8},{10,11... | collective-permute-start | bytes 2359304 | tf_op jit(solution)/shard_map/ppermute | solution.py:176
  74.1 26.0 %all-to-all-start.2 = ((bf16[64,8,128]{2,1,0:T(8,128)(2,1)}), bf16[64,8,128]{2,1,0:T(8,128)(2,1)S(1)}, u32[]{:S(2)}, u32[]{:S(2)}) async-start(bf16[64,8,128]{2,1,0:T(8,128)(2,1)} %get-tuple-element.14), calls=%async_computation.2 | async-start | bytes 262144 | tf_op jit(solution)/shard_map/all_to_all | solution.py:173

commit v3 on v2

--- a/solution.py
+++ b/solution.py
@@ -18,11 +18,7 @@
 def groups():
     dev = np.arange(1024).reshape(SIZES)
     whole = dev.transpose(0, 2, 1, 3, 4).reshape(8, 8, 8, 2)
-    near = [
-        np.array([[dev[pz + 2 * (t ^ (yh // 2 * 2 + x // 2)), yl, yh, 2 * x + px, c] for x in range(4)] for yh in range(4)]).reshape(-1)
-        for t in range(4)
-        for pz, yl, px, c in np.ndindex(2, 2, 2, 2)
-    ]
+    near = [dev[z, yl, :, px::2, c].reshape(-1) for c in range(2) for z in range(8) for yl in range(2) for px in range(2)]
     rest = [dev[pz::2, yl, :, px::2, c].reshape(-1) for c in range(2) for pz in range(2) for yl in range(2) for px in range(2)]
     cube = []
     for core in range(2):
@@ -55,7 +51,7 @@
     ]
     for read in reads:
         read.start()
-    source = lax.broadcasted_iota(jnp.int32, (768, 768), 0)
+    source = lax.broadcasted_iota(jnp.int32, (768, 1), 0)
     place = lax.broadcasted_iota(jnp.int32, (768, 768), 1)
     line = source // 12
     target = 12 * (32 * (line % 2) + 16 * (line // 2 % 2) + line // 4) + source % 12
@@ -104,7 +100,7 @@
     def _():
         copy.start()
 
-    row = lax.broadcasted_iota(jnp.int32, (256, SPAN), 0)
+    row = lax.broadcasted_iota(jnp.int32, (256, 1), 0)
     col = lax.broadcasted_iota(jnp.int32, (256, SPAN), 1)
     first = jnp.where(row % 8 < 6, 12 * (row // 8) + row % 8, -SPAN)
     pick = jnp.concatenate([(col == first).astype(F32), (col == first + 6).astype(F32)], axis=1).astype(BF)

time: 102 us -> 95.5 us (0.936)
  starting transfers between devices: 43.3 us -> 30.3 us
  blocking collectives: 19.3 us -> 29.3 us
  waiting for transfers between devices: 22.1 us -> 19.2 us
    all_to_all x2, starting transfers between devices: 37.3 us -> 20.9 us  [exchange(): lax.all_to_all(value, AXES, split_axis=0, concat_axis=0, axis_index_group...]
    all_to_all x1, blocking collectives: 19.3 us -> 29.3 us  [exchange(): lax.all_to_all(value, AXES, split_axis=0, concat_axis=0, axis_index_group...]
    ppermute x2, starting transfers between devices: 6 us -> 9.41 us  [swap(): return lax.ppermute(value, 'c', [(0, 1), (1, 0)])]
    all_to_all x2, waiting for transfers between devices: 20 us -> 17.1 us  [exchange(): lax.all_to_all(value, AXES, split_axis=0, concat_axis=0, axis_index_group...]
  transfers between devices with their start and end apart: 4 -> 4, of which waited for: 3 -> 3; matrix products, arithmetic and copies ran while one was open for 0% -> 0% of each run, Pallas kernels for 10% -> 11%
where the time goes in v3:
time: 95.5 us; the launch traced here: 95 us
  starting transfers between devices  30.3 us (32%)
  blocking collectives  29.3 us (31%)
  waiting for transfers between devices  19.2 us (20%)
  Pallas kernels  14.3 us (15%)
  local copies, waits for them, and re-layouts  1.14 us (1%)
    all_to_all x1, blocking collectives, exchange(): lax.all_to_all(value, AXES, split_axis=0, concat_axis=0, axis_index_group...  29.3 us
    all_to_all x2, starting transfers between devices, exchange(): lax.all_to_all(value, AXES, split_axis=0, concat_axis=0, axis_index_group...  20.9 us
    all_to_all x2, waiting for transfers between devices, exchange(): lax.all_to_all(value, AXES, split_axis=0, concat_axis=0, axis_index_group...  17.1 us
    ppermute x2, starting transfers between devices, swap(): return lax.ppermute(value, 'c', [(0, 1), (1, 0)])  9.41 us
    pallas_call x1, Pallas kernels, shards(): pl.pallas_call(term_kernel, out_shape=[jax.ShapeDtypeStruct((8, HD, 768),...  6.43 us
    pallas_call x1, Pallas kernels, shards(): pl.pallas_call(values_kernel, out_shape=jax.ShapeDtypeStruct((HD, TOK), B...  3.59 us
    ppermute x2, waiting for transfers between devices, swap(): return lax.ppermute(value, 'c', [(0, 1), (1, 0)])  2.1 us
  transfers between devices with their start and end apart: 4, of which 3 were waited for; matrix products, arithmetic and copies ran while one was open for 0% of the time, Pallas kernels for 11%

profile of v3, /device:TPU:1, one launch (start us, length us, event | category | flops | bytes accessed | tf_op | source)
XLA Modules:
  0.0 95.0 jit_solution(17446737026434662848)
XLA Ops:
  0.6 1.5 %scale.1 = bf16[16,16,192]{2,1,0:T(8,128)(2,1)} custom-call(s32[1]{0:T(128)} %bitcast.2.at_ref, bf16[64,192]{1,0:T(8,128)(2,1)} %codes_ref.1, f32[1,6]{1,0:T(1,128)} %scale_ref.1), custom_call_target="tpu_custom_call" | custom-call | tf_op jit(solution)/shard_map/scale/pallas_call | solution.py:176
  2.1 13.1 %all-to-all-start = ((bf16[16,16,192]{2,1,0:T(8,128)(2,1)}), bf16[16,16,192]{2,1,0:T(8,128)(2,1)S(1)}, u32[]{:S(2)}, u32[]{:S(2)}) async-start(bf16[16,16,192]{2,1,0:T(8,128)(2,1)} %scale.1), calls=%async_computation | async-start | bytes 262144 | tf_op jit(solution)/shard_map/all_to_all | solution.py:169
  15.3 6.4 %term.1 = (bf16[8,64,768]{2,1,0:T(8,128)(2,1)}, bf16[8,64,768]{2,1,0:T(8,128)(2,1)}) custom-call(s32[1]{0:T(128)} %bitcast.core_ref, bf16[128,12288]{1,0:T(8,128)(2,1)} %tokens_ref.1, bf16[64,128]{1,0:T(8,128)(2,1)} %bitcast.4), custom_call_target="tpu_custom_call" | custom-call | flops 201326592 | bytes 5242880 | tf_op jit(solution)/shard_map/term/pallas_call | solution.py:185
  21.7 5.0 %all-to-all-done.near_ref = bf16[16,16,192]{2,1,0:T(8,128)(2,1)S(1)} async-done(((bf16[16,16,192]{2,1,0:T(8,128)(2,1)}), bf16[16,16,192]{2,1,0:T(8,128)(2,1)S(1)}, u32[]{:S(2)}, u32[]{:S(2)}) %all-to-all-start) | async-done | bytes 98336 | tf_op jit(solution)/shard_map/all_to_all | solution.py:169
  26.7 7.5 %collective-permute-start = (bf16[8,64,768]{2,1,0:T(8,128)(2,1)}, bf16[8,64,768]{2,1,0:T(8,128)(2,1)S(1)}, u32[]{:S(2)}, u32[]{:S(2)}) collective-permute-start(bf16[8,64,768]{2,1,0:T(8,128)(2,1)} %get-tuple-element.13), channel_id=1, source_target_pairs={{0,1},{1,0},{2,3},{3,2},{4,5},{5,4},{6,7},{7,6},{8,9},{9,8},{10,11... | collective-permute-start | bytes 2359304 | tf_op jit(solution)/shard_map/ppermute | solution.py:172
  34.2 2.1 %collective-permute-done.other_ref = bf16[8,64,768]{2,1,0:T(8,128)(2,1)S(1)} collective-permute-done((bf16[8,64,768]{2,1,0:T(8,128)(2,1)}, bf16[8,64,768]{2,1,0:T(8,128)(2,1)S(1)}, u32[]{:S(2)}, u32[]{:S(2)}) %collective-permute-start) | collective-permute-done | bytes 786464 | tf_op jit(solution)/shard_map/ppermute | solution.py:172
  36.3 0.0 copy-start.1
  36.3 1.1 %copy-done.1 = bf16[8,64,768]{2,1,0:T(8,128)(2,1)S(1)} copy-done((bf16[8,64,768]{2,1,0:T(8,128)(2,1)S(1)}, bf16[8,64,768]{2,1,0:T(8,128)(2,1)}, u32[]{:S(2)}) %copy-start.1) | copy-done | bytes 786456
  37.4 0.5 fill.1
  37.9 29.3 %all_to_all.15.in_ref.in_hbm = bf16[8,64,1536]{2,1,0:T(8,128)(2,1)S(1)} all-to-all(bf16[8,64,1536]{2,1,0:T(8,128)(2,1)S(1)} %fill.1), channel_id=1, replica_groups={{0,2,64,66,128,130,192,194},{4,6,68,70,132,134,196,198},{8,10,72,74,136..., dimensions={0} | all-to-all | bytes 3145728 | tf_op jit(solution)/shard_map/all_to_all | solution.py:169
  67.2 0.0 copy-start
  67.2 1.6 %sum.1 = (bf16[64,8,128]{2,1,0:T(8,128)(2,1)}, bf16[8,64,768]{2,1,0:T(8,128)(2,1)}) custom-call(bf16[8,64,1536]{2,1,0:T(8,128)(2,1)S(1)} %all_to_all.15.in_ref.in_hbm, bf16[8,64,1536]{2,1,0:T(8,128)(2,1)S(1)} %all_to_all.15.in_ref.in_hbm), custom_call_target="tpu_custom_call" | custom-call | flops 1572864 | bytes 2097152 | tf_op jit(solution)/shard_map/sum/pallas_call | solution.py:213
  68.8 1.9 %collective-permute-start.1 = (bf16[8,64,768]{2,1,0:T(8,128)(2,1)}, bf16[8,64,768]{2,1,0:T(8,128)(2,1)}, u32[]{:S(2)}, u32[]{:S(2)}) collective-permute-start(bf16[8,64,768]{2,1,0:T(8,128)(2,1)} %get-tuple-element.15.own_ref), channel_id=1, source_target_pairs={{0,1},{1,0},{2,3},{3,2},{4,5},{5,4},{6,7},{7,6},{8,9},{9,8},{10,11... | collective-permute-start | bytes 2359304 | tf_op jit(solution)/shard_map/ppermute | solution.py:172
  70.8 7.8 %all-to-all-start.2 = ((bf16[64,8,128]{2,1,0:T(8,128)(2,1)}), bf16[64,8,128]{2,1,0:T(8,128)(2,1)S(1)}, u32[]{:S(2)}, u32[]{:S(2)}) async-start(bf16[64,8,128]{2,1,0:T(8,128)(2,1)} %get-tuple-element.14), calls=%async_computation.2 | async-start | bytes 262144 | tf_op jit(solution)/shard_map/all_to_all | solution.py:169
  78.5 0.0 collective-permute-done.1.other_ref
  78.5 0.0 copy-done
  78.6 3.6 %values.1 = bf16[64,128]{1,0:T(8,128)(2,1)} custom-call(s32[1]{0:T(128)} %bitcast.core_ref, bf16[8,64,768]{2,1,0:T(8,128)(2,1)} %get-tuple-element.15.own_ref, bf16[8,64,768]{2,1,0:T(8,128)(2,1)} %collective-permute-done.1.other_ref, bf16[128,12288]{1,0:T(8,128)(2,1)S(1)} %copy-done), custom_call_target="tpu_custom_call" | custom-call | flops 201326592 | bytes 5242880 | tf_op jit(solution)/shard_map/values/pallas_call | solution.py:225
  82.1 12.1 %all-to-all-done.2.in_ref = bf16[64,8,128]{2,1,0:T(8,128)(2,1)S(1)} async-done(((bf16[64,8,128]{2,1,0:T(8,128)(2,1)}), bf16[64,8,128]{2,1,0:T(8,128)(2,1)S(1)}, u32[]{:S(2)}, u32[]{:S(2)}) %all-to-all-start.2) | async-done | bytes 131104 | tf_op jit(solution)/shard_map/all_to_all | solution.py:169
  94.3 0.7 final.1
Async XLA Ops:
  2.1 24.6 %all-to-all-start = ((bf16[16,16,192]{2,1,0:T(8,128)(2,1)}), bf16[16,16,192]{2,1,0:T(8,128)(2,1)S(1)}, u32[]{:S(2)}, u32[]{:S(2)}) async-start(bf16[16,16,192]{2,1,0:T(8,128)(2,1)} %scale.1), calls=%async_computation | async-start | bytes 262144 | tf_op jit(solution)/shard_map/all_to_all | solution.py:169
  26.7 9.6 %collective-permute-start = (bf16[8,64,768]{2,1,0:T(8,128)(2,1)}, bf16[8,64,768]{2,1,0:T(8,128)(2,1)S(1)}, u32[]{:S(2)}, u32[]{:S(2)}) collective-permute-start(bf16[8,64,768]{2,1,0:T(8,128)(2,1)} %get-tuple-element.13), channel_id=1, source_target_pairs={{0,1},{1,0},{2,3},{3,2},{4,5},{5,4},{6,7},{7,6},{8,9},{9,8},{10,11... | collective-permute-start | bytes 2359304 | tf_op jit(solution)/shard_map/ppermute | solution.py:172
  36.3 1.1 %copy-start.1 = (bf16[8,64,768]{2,1,0:T(8,128)(2,1)S(1)}, bf16[8,64,768]{2,1,0:T(8,128)(2,1)}, u32[]{:S(2)}) copy-start(bf16[8,64,768]{2,1,0:T(8,128)(2,1)} %get-tuple-element.12.own_ref) | copy-start | bytes 2359300
  67.2 11.4 %copy-start = (bf16[128,12288]{1,0:T(8,128)(2,1)S(1)}, bf16[128,12288]{1,0:T(8,128)(2,1)}, u32[]{:S(2)}) copy-start(bf16[128,12288]{1,0:T(8,128)(2,1)} %tokens_ref.1) | copy-start | bytes 9437188
  68.8 9.7 %collective-permute-start.1 = (bf16[8,64,768]{2,1,0:T(8,128)(2,1)}, bf16[8,64,768]{2,1,0:T(8,128)(2,1)}, u32[]{:S(2)}, u32[]{:S(2)}) collective-permute-start(bf16[8,64,768]{2,1,0:T(8,128)(2,1)} %get-tuple-element.15.own_ref), channel_id=1, source_target_pairs={{0,1},{1,0},{2,3},{3,2},{4,5},{5,4},{6,7},{7,6},{8,9},{9,8},{10,11... | collective-permute-start | bytes 2359304 | tf_op jit(solution)/shard_map/ppermute | solution.py:172
  70.8 23.5 %all-to-all-start.2 = ((bf16[64,8,128]{2,1,0:T(8,128)(2,1)}), bf16[64,8,128]{2,1,0:T(8,128)(2,1)S(1)}, u32[]{:S(2)}, u32[]{:S(2)}) async-start(bf16[64,8,128]{2,1,0:T(8,128)(2,1)} %get-tuple-element.14), calls=%async_computation.2 | async-start | bytes 262144 | tf_op jit(solution)/shard_map/all_to_all | solution.py:169

commit v4 on v3

--- a/solution.py
+++ b/solution.py
@@ -10,6 +10,7 @@
 AXES = ("z", "yl", "yh", "x", "c")
 SIZES = (8, 2, 4, 8, 2)
 D, HD, TOK = 12288, 64, 128
+SHARE = 2
 BF, F32 = jnp.bfloat16, jnp.float32
 NT = (((1,), (1,)), ((), ()))
 SPAN = 384
@@ -92,13 +93,18 @@
             out_ref[p, 16 * (k // 4) : 16 * (k // 4 + 1), 768 + 192 * (k % 4) : 960 + 192 * (k % 4)] = near_ref[k]
 
 
-def sum_kernel(in_ref, in_hbm, out_ref, weights_hbm, sem):
+def sum_kernel(in_ref, in_hbm, out_ref, *refs):
     step = pl.program_id(0)
-    copy = pltpu.make_async_copy(in_hbm.at[:, :, pl.ds(768, 768)], weights_hbm, sem)
+    weights, sem = refs[:-1], refs[-1]
+    copies = [
+        pltpu.make_async_copy(in_hbm.at[pl.ds(SHARE * i, SHARE), :, pl.ds(768, 768)], piece, sem.at[i])
+        for i, piece in enumerate(weights)
+    ]
 
     @pl.when(step == 0)
     def _():
-        copy.start()
+        for copy in copies:
+            copy.start()
 
     row = lax.broadcasted_iota(jnp.int32, (256, 1), 0)
     col = lax.broadcasted_iota(jnp.int32, (256, SPAN), 1)
@@ -117,11 +123,15 @@
 
     @pl.when(step == 1)
     def _():
-        copy.wait()
-
-
-def values_kernel(core_ref, own_ref, other_ref, tokens_ref, out_ref):
-    def product(first_ref, second_ref):
+        for copy in copies:
+            copy.wait()
+
+
+def values_kernel(core_ref, *refs):
+    tokens_ref, out_ref = refs[-2:]
+    own, other = refs[: 8 // SHARE], refs[8 // SHARE : -2]
+
+    def product(first, second):
         total = jnp.zeros((HD, TOK), F32)
         for yh in range(4):
             for x in range(8):
@@ -129,12 +139,12 @@
                 halves = [
                     jnp.concatenate(
                         [
-                            ref[2 * q + x % 2, 16 * yh : 16 * (yh + 1), 192 * (x // 2) : 192 * (x // 2 + 1)]
+                            pieces[(2 * q + x % 2) // SHARE][(2 * q + x % 2) % SHARE, 16 * yh : 16 * (yh + 1), 192 * (x // 2) : 192 * (x // 2 + 1)]
                             for q in range(4)
                         ],
                         axis=0,
                     )
-                    for ref in (first_ref, second_ref)
+                    for pieces in (first, second)
                 ]
                 total += lax.dot_general(
                     jnp.concatenate(halves, axis=1), tokens_ref[:, at : at + SPAN], NT, preferred_element_type=F32
@@ -143,11 +153,11 @@
 
     @pl.when(core_ref[0] == 0)
     def _():
-        product(own_ref, other_ref)
+        product(own, other)
 
     @pl.when(core_ref[0] != 0)
     def _():
-        product(other_ref, own_ref)
+        product(other, own)
 
 
 def final_kernel(in_ref, out_ref):
@@ -210,13 +220,13 @@
         name="fill",
     )(near, own, swap(send))
     arrived = exchange(outgoing, cube)
-    partial_sum, weights = pl.pallas_call(
+    partial_sum, *weights = pl.pallas_call(
         sum_kernel,
         grid=(2,),
-        out_shape=(jax.ShapeDtypeStruct((64, 8, 128), BF), jax.ShapeDtypeStruct((8, HD, 768), BF)),
+        out_shape=[jax.ShapeDtypeStruct((64, 8, 128), BF)] + [jax.ShapeDtypeStruct((SHARE, HD, 768), BF)] * (8 // SHARE),
         in_specs=[pl.BlockSpec((8, HD, SPAN), lambda i: (0, 0, i)), hbm],
-        out_specs=(pl.BlockSpec((32, 8, 128), lambda i: (i, 0, 0)), hbm),
-        scratch_shapes=[pltpu.SemaphoreType.DMA],
+        out_specs=[pl.BlockSpec((32, 8, 128), lambda i: (i, 0, 0))] + [hbm] * (8 // SHARE),
+        scratch_shapes=[pltpu.SemaphoreType.DMA((8 // SHARE,))],
         compiler_params=pltpu.CompilerParams(vmem_limit_bytes=40 * 2**20),
         cost_estimate=pl.CostEstimate(flops=2 * D * HD, bytes_accessed=2 * 2**20, transcendentals=0),
         name="sum",
@@ -225,12 +235,12 @@
     values = pl.pallas_call(
         values_kernel,
         out_shape=jax.ShapeDtypeStruct((HD, TOK), BF),
-        in_specs=[smem, vmem, vmem, vmem],
+        in_specs=[smem] + [vmem] * (16 // SHARE + 1),
         out_specs=vmem,
-        compiler_params=pltpu.CompilerParams(vmem_limit_bytes=40 * 2**20),
+        compiler_params=pltpu.CompilerParams(vmem_limit_bytes=52 * 2**20),
         cost_estimate=pl.CostEstimate(flops=2 * D * TOK * HD, bytes_accessed=5 * 2**20, transcendentals=0),
         name="values",
-    )(core, weights, swap(weights), tokens)
+    )(core, *weights, *[swap(piece) for piece in weights], tokens)
     last, values = lax.optimization_barrier((last, values))
     weight_grad = pl.pallas_call(
         final_kernel,

time: 95.5 us -> 93.5 us (0.979)
  waiting for transfers between devices: 19.2 us -> 9.95 us
  starting transfers between devices: 30.3 us -> 37 us
    all_to_all x2, waiting for transfers between devices: 17.1 us -> 6.83 us  [exchange(): lax.all_to_all(value, AXES, split_axis=0, concat_axis=0, axis_index_group...]
    ppermute x2 -> x5, starting transfers between devices: 9.41 us -> 16.1 us  [swap(): return lax.ppermute(value, 'c', [(0, 1), (1, 0)])]
    ppermute x2 -> x5, waiting for transfers between devices: 2.1 us -> 3.13 us  [swap(): return lax.ppermute(value, 'c', [(0, 1), (1, 0)])]
  transfers between devices with their start and end apart: 4 -> 7, of which waited for: 3 -> 4; matrix products, arithmetic and copies ran while one was open for 0% -> 0% of each run, Pallas kernels for 11% -> 11%
where the time goes in v4:
time: 93.5 us; the launch traced here: 92.9 us
  starting transfers between devices  37 us (40%)
  blocking collectives  29.3 us (31%)
  Pallas kernels  14.7 us (16%)
  waiting for transfers between devices  9.95 us (11%)
  local copies, waits for them, and re-layouts  1.13 us (1%)
    all_to_all x1, blocking collectives, exchange(): lax.all_to_all(value, AXES, split_axis=0, concat_axis=0, axis_index_group...  29.3 us
    all_to_all x2, starting transfers between devices, exchange(): lax.all_to_all(value, AXES, split_axis=0, concat_axis=0, axis_index_group...  20.9 us
    ppermute x5, starting transfers between devices, swap(): return lax.ppermute(value, 'c', [(0, 1), (1, 0)])  16.1 us
    all_to_all x2, waiting for transfers between devices, exchange(): lax.all_to_all(value, AXES, split_axis=0, concat_axis=0, axis_index_group...  6.83 us
    pallas_call x1, Pallas kernels, shards(): pl.pallas_call(term_kernel, out_shape=[jax.ShapeDtypeStruct((8, HD, 768),...  6.48 us
    pallas_call x1, Pallas kernels, shards(): pl.pallas_call(values_kernel, out_shape=jax.ShapeDtypeStruct((HD, TOK), B...  4.1 us
    ppermute x5, waiting for transfers between devices, swap(): return lax.ppermute(value, 'c', [(0, 1), (1, 0)])  3.13 us
  transfers between devices with their start and end apart: 7, of which 4 were waited for; matrix products, arithmetic and copies ran while one was open for 0% of the time, Pallas kernels for 11%

profile of v4, /device:TPU:1, one launch (start us, length us, event | category | flops | bytes accessed | tf_op | source)
XLA Modules:
  0.0 92.9 jit_solution(17254209690819043588)
XLA Ops:
  0.6 1.5 %scale.1 = bf16[16,16,192]{2,1,0:T(8,128)(2,1)} custom-call(s32[1]{0:T(128)} %bitcast.2.at_ref, bf16[64,192]{1,0:T(8,128)(2,1)} %codes_ref.1, f32[1,6]{1,0:T(1,128)} %scale_ref.1), custom_call_target="tpu_custom_call" | custom-call | tf_op jit(solution)/shard_map/scale/pallas_call | solution.py:186
  2.1 13.1 %all-to-all-start = ((bf16[16,16,192]{2,1,0:T(8,128)(2,1)}), bf16[16,16,192]{2,1,0:T(8,128)(2,1)S(1)}, u32[]{:S(2)}, u32[]{:S(2)}) async-start(bf16[16,16,192]{2,1,0:T(8,128)(2,1)} %scale.1), calls=%async_computation | async-start | bytes 262144 | tf_op jit(solution)/shard_map/all_to_all | solution.py:179
  15.3 6.5 %term.1 = (bf16[8,64,768]{2,1,0:T(8,128)(2,1)}, bf16[8,64,768]{2,1,0:T(8,128)(2,1)}) custom-call(s32[1]{0:T(128)} %bitcast.core_ref, bf16[128,12288]{1,0:T(8,128)(2,1)} %refs_8_.1, bf16[64,128]{1,0:T(8,128)(2,1)} %bitcast.4), custom_call_target="tpu_custom_call" | custom-call | flops 201326592 | bytes 5242880 | tf_op jit(solution)/shard_map/term/pallas_call | solution.py:195
  21.7 4.9 %all-to-all-done.near_ref = bf16[16,16,192]{2,1,0:T(8,128)(2,1)S(1)} async-done(((bf16[16,16,192]{2,1,0:T(8,128)(2,1)}), bf16[16,16,192]{2,1,0:T(8,128)(2,1)S(1)}, u32[]{:S(2)}, u32[]{:S(2)}) %all-to-all-start) | async-done | bytes 98336 | tf_op jit(solution)/shard_map/all_to_all | solution.py:179
  26.7 7.5 %collective-permute-start = (bf16[8,64,768]{2,1,0:T(8,128)(2,1)}, bf16[8,64,768]{2,1,0:T(8,128)(2,1)S(1)}, u32[]{:S(2)}, u32[]{:S(2)}) collective-permute-start(bf16[8,64,768]{2,1,0:T(8,128)(2,1)} %get-tuple-element.16), channel_id=1, source_target_pairs={{0,1},{1,0},{2,3},{3,2},{4,5},{5,4},{6,7},{7,6},{8,9},{9,8},{10,11... | collective-permute-start | bytes 2359304 | tf_op jit(solution)/shard_map/ppermute | solution.py:182
  34.2 2.1 %collective-permute-done.other_ref = bf16[8,64,768]{2,1,0:T(8,128)(2,1)S(1)} collective-permute-done((bf16[8,64,768]{2,1,0:T(8,128)(2,1)}, bf16[8,64,768]{2,1,0:T(8,128)(2,1)S(1)}, u32[]{:S(2)}, u32[]{:S(2)}) %collective-permute-start) | collective-permute-done | bytes 786464 | tf_op jit(solution)/shard_map/ppermute | solution.py:182
  36.3 0.0 copy-start
  36.3 1.1 %copy-done = bf16[8,64,768]{2,1,0:T(8,128)(2,1)S(1)} copy-done((bf16[8,64,768]{2,1,0:T(8,128)(2,1)S(1)}, bf16[8,64,768]{2,1,0:T(8,128)(2,1)}, u32[]{:S(2)}) %copy-start) | copy-done | bytes 786456
  37.4 0.5 fill.1
  37.9 29.3 %all_to_all.15.in_ref.in_hbm = bf16[8,64,1536]{2,1,0:T(8,128)(2,1)S(1)} all-to-all(bf16[8,64,1536]{2,1,0:T(8,128)(2,1)S(1)} %fill.1), channel_id=1, replica_groups={{0,2,64,66,128,130,192,194},{4,6,68,70,132,134,196,198},{8,10,72,74,136..., dimensions={0} | all-to-all | bytes 3145728 | tf_op jit(solution)/shard_map/all_to_all | solution.py:179
  67.2 1.4 %sum.1 = (bf16[64,8,128]{2,1,0:T(8,128)(2,1)}, bf16[2,64,768]{2,1,0:T(8,128)(2,1)S(1)}, bf16[2,64,768]{2,1,0:T(8,128)(2,1)S(1)}, bf16[2,64,768]{2,1,0:T(8,128)(2,1)S(1)}, bf16[2,64,768]{2,1,0:T(8,128)(2,1)S(1)}) custom-call(bf16[8,64,1536]{2,1,0:T(8,128)(2,1)S(1)} %all_to_all.15.in_ref.in_hbm, bf16[8,64,1536]{2,1,0:T(8,128)(2,1)S(1)} %all_to_all.15.in_ref.in_hbm), custom_call_target="tpu_custom_call" | custom-call | flops 1572864 | bytes 2097152 | tf_op jit(solution)/shard_map/sum/pallas_call | solution.py:223
  68.6 7.8 %all-to-all-start.2 = ((bf16[64,8,128]{2,1,0:T(8,128)(2,1)}), bf16[64,8,128]{2,1,0:T(8,128)(2,1)S(1)}, u32[]{:S(2)}, u32[]{:S(2)}) async-start(bf16[64,8,128]{2,1,0:T(8,128)(2,1)} %get-tuple-element.17), calls=%async_computation.2 | async-start | bytes 262144 | tf_op jit(solution)/shard_map/all_to_all | solution.py:179
  76.4 1.9 %collective-permute-start.1 = (bf16[2,64,768]{2,1,0:T(8,128)(2,1)S(1)}, bf16[2,64,768]{2,1,0:T(8,128)(2,1)S(1)}, u32[]{:S(2)}, u32[]{:S(2)}) collective-permute-start(bf16[2,64,768]{2,1,0:T(8,128)(2,1)S(1)} %get-tuple-element.18.refs_0_), channel_id=1, source_target_pairs={{0,1},{1,0},{2,3},{3,2},{4,5},{5,4},{6,7},{7,6},{8,9},{9,8},{10,11... | collective-permute-start | bytes 589832 | tf_op jit(solution)/shard_map/ppermute | solution.py:182
  78.3 2.4 %collective-permute-start.2 = (bf16[2,64,768]{2,1,0:T(8,128)(2,1)S(1)}, bf16[2,64,768]{2,1,0:T(8,128)(2,1)S(1)}, u32[]{:S(2)}, u32[]{:S(2)}) collective-permute-start(bf16[2,64,768]{2,1,0:T(8,128)(2,1)S(1)} %get-tuple-element.19.refs_1_), channel_id=1, source_target_pairs={{0,1},{1,0},{2,3},{3,2},{4,5},{5,4},{6,7},{7,6},{8,9},{9,8},{10,11... | collective-permute-start | bytes 589832 | tf_op jit(solution)/shard_map/ppermute | solution.py:182
  80.8 1.9 %collective-permute-start.3 = (bf16[2,64,768]{2,1,0:T(8,128)(2,1)S(1)}, bf16[2,64,768]{2,1,0:T(8,128)(2,1)S(1)}, u32[]{:S(2)}, u32[]{:S(2)}) collective-permute-start(bf16[2,64,768]{2,1,0:T(8,128)(2,1)S(1)} %get-tuple-element.20.refs_2_), channel_id=1, source_target_pairs={{0,1},{1,0},{2,3},{3,2},{4,5},{5,4},{6,7},{7,6},{8,9},{9,8},{10,11... | collective-permute-start | bytes 589832 | tf_op jit(solution)/shard_map/ppermute | solution.py:182
  82.7 2.4 %collective-permute-start.4 = (bf16[2,64,768]{2,1,0:T(8,128)(2,1)S(1)}, bf16[2,64,768]{2,1,0:T(8,128)(2,1)S(1)}, u32[]{:S(2)}, u32[]{:S(2)}) collective-permute-start(bf16[2,64,768]{2,1,0:T(8,128)(2,1)S(1)} %get-tuple-element.21.refs_3_), channel_id=1, source_target_pairs={{0,1},{1,0},{2,3},{3,2},{4,5},{5,4},{6,7},{7,6},{8,9},{9,8},{10,11... | collective-permute-start | bytes 589832 | tf_op jit(solution)/shard_map/ppermute | solution.py:182
  85.1 0.0 collective-permute-done.1.refs_4_
  85.1 0.0 collective-permute-done.2.refs_5_
  85.1 0.0 collective-permute-done.3.refs_6_
  85.1 1.0 %collective-permute-done.4.refs_7_ = bf16[2,64,768]{2,1,0:T(8,128)(2,1)S(1)} collective-permute-done((bf16[2,64,768]{2,1,0:T(8,128)(2,1)S(1)}, bf16[2,64,768]{2,1,0:T(8,128)(2,1)S(1)}, u32[]{:S(2)}, u32[]{:S(2)}) %collective-permute-start.4) | collective-permute-done | bytes 196640 | tf_op jit(solution)/shard_map/ppermute | solution.py:182
  86.1 4.1 %values.1 = bf16[64,128]{1,0:T(8,128)(2,1)} custom-call(s32[1]{0:T(128)} %bitcast.core_ref, bf16[2,64,768]{2,1,0:T(8,128)(2,1)S(1)} %get-tuple-element.18.refs_0_, bf16[2,64,768]{2,1,0:T(8,128)(2,1)S(1)} %get-tuple-element.19.refs_1_, bf16[2,64,768]{2,1,0:T(8,128)(2,1)S(1)} %get-tuple-element.20.refs_2_, bf16[2,64,768]{2,1,0:T(8,128)(2,1)S(1)} %get-tuple-element.21.refs_3_, ...), custom_call_target="tpu_custom_call" | custom-call | flops 201326592 | bytes 5242880 | tf_op jit(solution)/shard_map/values/pallas_call | solution.py:235
  90.2 1.9 %all-to-all-done.2.in_ref = bf16[64,8,128]{2,1,0:T(8,128)(2,1)S(1)} async-done(((bf16[64,8,128]{2,1,0:T(8,128)(2,1)}), bf16[64,8,128]{2,1,0:T(8,128)(2,1)S(1)}, u32[]{:S(2)}, u32[]{:S(2)}) %all-to-all-start.2) | async-done | bytes 131104 | tf_op jit(solution)/shard_map/all_to_all | solution.py:179
  92.1 0.7 final.1
Async XLA Ops:
  2.1 24.6 %all-to-all-start = ((bf16[16,16,192]{2,1,0:T(8,128)(2,1)}), bf16[16,16,192]{2,1,0:T(8,128)(2,1)S(1)}, u32[]{:S(2)}, u32[]{:S(2)}) async-start(bf16[16,16,192]{2,1,0:T(8,128)(2,1)} %scale.1), calls=%async_computation | async-start | bytes 262144 | tf_op jit(solution)/shard_map/all_to_all | solution.py:179
  26.7 9.6 %collective-permute-start = (bf16[8,64,768]{2,1,0:T(8,128)(2,1)}, bf16[8,64,768]{2,1,0:T(8,128)(2,1)S(1)}, u32[]{:S(2)}, u32[]{:S(2)}) collective-permute-start(bf16[8,64,768]{2,1,0:T(8,128)(2,1)} %get-tuple-element.16), channel_id=1, source_target_pairs={{0,1},{1,0},{2,3},{3,2},{4,5},{5,4},{6,7},{7,6},{8,9},{9,8},{10,11... | collective-permute-start | bytes 2359304 | tf_op jit(solution)/shard_map/ppermute | solution.py:182
  36.3 1.1 %copy-start = (bf16[8,64,768]{2,1,0:T(8,128)(2,1)S(1)}, bf16[8,64,768]{2,1,0:T(8,128)(2,1)}, u32[]{:S(2)}) copy-start(bf16[8,64,768]{2,1,0:T(8,128)(2,1)} %get-tuple-element.15.own_ref) | copy-start | bytes 2359300
  68.6 23.5 %all-to-all-start.2 = ((bf16[64,8,128]{2,1,0:T(8,128)(2,1)}), bf16[64,8,128]{2,1,0:T(8,128)(2,1)S(1)}, u32[]{:S(2)}, u32[]{:S(2)}) async-start(bf16[64,8,128]{2,1,0:T(8,128)(2,1)} %get-tuple-element.17), calls=%async_computation.2 | async-start | bytes 262144 | tf_op jit(solution)/shard_map/all_to_all | solution.py:179
  76.4 8.7 %collective-permute-start.1 = (bf16[2,64,768]{2,1,0:T(8,128)(2,1)S(1)}, bf16[2,64,768]{2,1,0:T(8,128)(2,1)S(1)}, u32[]{:S(2)}, u32[]{:S(2)}) collective-permute-start(bf16[2,64,768]{2,1,0:T(8,128)(2,1)S(1)} %get-tuple-element.18.refs_0_), channel_id=1, source_target_pairs={{0,1},{1,0},{2,3},{3,2},{4,5},{5,4},{6,7},{7,6},{8,9},{9,8},{10,11... | collective-permute-start | bytes 589832 | tf_op jit(solution)/shard_map/ppermute | solution.py:182
  78.3 6.8 %collective-permute-start.2 = (bf16[2,64,768]{2,1,0:T(8,128)(2,1)S(1)}, bf16[2,64,768]{2,1,0:T(8,128)(2,1)S(1)}, u32[]{:S(2)}, u32[]{:S(2)}) collective-permute-start(bf16[2,64,768]{2,1,0:T(8,128)(2,1)S(1)} %get-tuple-element.19.refs_1_), channel_id=1, source_target_pairs={{0,1},{1,0},{2,3},{3,2},{4,5},{5,4},{6,7},{7,6},{8,9},{9,8},{10,11... | collective-permute-start | bytes 589832 | tf_op jit(solution)/shard_map/ppermute | solution.py:182
  80.8 4.4 %collective-permute-start.3 = (bf16[2,64,768]{2,1,0:T(8,128)(2,1)S(1)}, bf16[2,64,768]{2,1,0:T(8,128)(2,1)S(1)}, u32[]{:S(2)}, u32[]{:S(2)}) collective-permute-start(bf16[2,64,768]{2,1,0:T(8,128)(2,1)S(1)} %get-tuple-element.20.refs_2_), channel_id=1, source_target_pairs={{0,1},{1,0},{2,3},{3,2},{4,5},{5,4},{6,7},{7,6},{8,9},{9,8},{10,11... | collective-permute-start | bytes 589832 | tf_op jit(solution)/shard_map/ppermute | solution.py:182
  82.7 3.5 %collective-permute-start.4 = (bf16[2,64,768]{2,1,0:T(8,128)(2,1)S(1)}, bf16[2,64,768]{2,1,0:T(8,128)(2,1)S(1)}, u32[]{:S(2)}, u32[]{:S(2)}) collective-permute-start(bf16[2,64,768]{2,1,0:T(8,128)(2,1)S(1)} %get-tuple-element.21.refs_3_), channel_id=1, source_target_pairs={{0,1},{1,0},{2,3},{3,2},{4,5},{5,4},{6,7},{7,6},{8,9},{9,8},{10,11... | collective-permute-start | bytes 589832 | tf_op jit(solution)/shard_map/ppermute | solution.py:182

commit v5 on v4

--- a/solution.py
+++ b/solution.py
@@ -86,6 +86,12 @@
         write.wait()
 
 
+def keep_kernel(in_hbm, out_ref, sem):
+    copy = pltpu.make_async_copy(in_hbm, out_ref, sem)
+    copy.start()
+    copy.wait()
+
+
 def fill_kernel(near_ref, own_ref, other_ref, out_ref):
     out_ref[:, :, :768] = (own_ref[...].astype(F32) + other_ref[...].astype(F32)).astype(BF)
     for p in range(out_ref.shape[0]):
@@ -209,6 +215,16 @@
         name="term",
     )(core, tokens, upstream.T)
     send, near = lax.optimization_barrier((send, near))
+    own = pl.pallas_call(
+        keep_kernel,
+        out_shape=jax.ShapeDtypeStruct((8, HD, 768), BF),
+        in_specs=[hbm],
+        out_specs=vmem,
+        scratch_shapes=[pltpu.SemaphoreType.DMA],
+        compiler_params=pltpu.CompilerParams(vmem_limit_bytes=8 * 2**20),
+        cost_estimate=pl.CostEstimate(flops=0, bytes_accessed=4 * 2**20, transcendentals=0),
+        name="keep",
+    )(own)
     part = pl.BlockSpec((4, HD, 768), lambda i: (i, 0, 0))
     outgoing = pl.pallas_call(
         fill_kernel,

time: 93.5 us -> 92.4 us (0.988)
  waiting for transfers between devices: 9.95 us -> 8.75 us
    ppermute x5, waiting for transfers between devices: 3.13 us -> 1.92 us  [swap(): return lax.ppermute(value, 'c', [(0, 1), (1, 0)])]
  transfers between devices with their start and end apart: 7 -> 7, of which waited for: 4 -> 4; matrix products, arithmetic and copies ran while one was open for 0% -> 0% of each run, Pallas kernels for 11% -> 12%
where the time goes in v5:
time: 92.4 us; the launch traced here: 91.7 us
  starting transfers between devices  37 us (40%)
  blocking collectives  29.3 us (32%)
  Pallas kernels  14.8 us (16%)
  waiting for transfers between devices  8.75 us (9%)
  local copies, waits for them, and re-layouts  1.13 us (1%)
    all_to_all x1, blocking collectives, exchange(): lax.all_to_all(value, AXES, split_axis=0, concat_axis=0, axis_index_group...  29.3 us
    all_to_all x2, starting transfers between devices, exchange(): lax.all_to_all(value, AXES, split_axis=0, concat_axis=0, axis_index_group...  20.9 us
    ppermute x5, starting transfers between devices, swap(): return lax.ppermute(value, 'c', [(0, 1), (1, 0)])  16.1 us
    all_to_all x2, waiting for transfers between devices, exchange(): lax.all_to_all(value, AXES, split_axis=0, concat_axis=0, axis_index_group...  6.83 us
    pallas_call x1, Pallas kernels, shards(): pl.pallas_call(term_kernel, out_shape=[jax.ShapeDtypeStruct((8, HD, 768),...  6.48 us
    pallas_call x1, Pallas kernels, shards(): pl.pallas_call(values_kernel, out_shape=jax.ShapeDtypeStruct((HD, TOK), B...  4.1 us
    ppermute x5, waiting for transfers between devices, swap(): return lax.ppermute(value, 'c', [(0, 1), (1, 0)])  1.92 us
  transfers between devices with their start and end apart: 7, of which 4 were waited for; matrix products, arithmetic and copies ran while one was open for 0% of the time, Pallas kernels for 12%

profile of v5, /device:TPU:1, one launch (start us, length us, event | category | flops | bytes accessed | tf_op | source)
XLA Modules:
  0.0 91.7 jit_solution(4352971709057215166)
XLA Ops:
  0.6 1.5 %scale.1 = bf16[16,16,192]{2,1,0:T(8,128)(2,1)} custom-call(s32[1]{0:T(128)} %bitcast.2.at_ref, bf16[64,192]{1,0:T(8,128)(2,1)} %codes_ref.1, f32[1,6]{1,0:T(1,128)} %scale_ref.1), custom_call_target="tpu_custom_call" | custom-call | tf_op jit(solution)/shard_map/scale/pallas_call | solution.py:192
  2.1 13.1 %all-to-all-start = ((bf16[16,16,192]{2,1,0:T(8,128)(2,1)}), bf16[16,16,192]{2,1,0:T(8,128)(2,1)S(1)}, u32[]{:S(2)}, u32[]{:S(2)}) async-start(bf16[16,16,192]{2,1,0:T(8,128)(2,1)} %scale.1), calls=%async_computation | async-start | bytes 262144 | tf_op jit(solution)/shard_map/all_to_all | solution.py:185
  15.3 6.5 %term.1 = (bf16[8,64,768]{2,1,0:T(8,128)(2,1)}, bf16[8,64,768]{2,1,0:T(8,128)(2,1)}) custom-call(s32[1]{0:T(128)} %bitcast.core_ref, bf16[128,12288]{1,0:T(8,128)(2,1)} %refs_8_.1, bf16[64,128]{1,0:T(8,128)(2,1)} %bitcast.4), custom_call_target="tpu_custom_call" | custom-call | flops 201326592 | bytes 5242880 | tf_op jit(solution)/shard_map/term/pallas_call | solution.py:201
  21.7 4.9 %all-to-all-done.near_ref = bf16[16,16,192]{2,1,0:T(8,128)(2,1)S(1)} async-done(((bf16[16,16,192]{2,1,0:T(8,128)(2,1)}), bf16[16,16,192]{2,1,0:T(8,128)(2,1)S(1)}, u32[]{:S(2)}, u32[]{:S(2)}) %all-to-all-start) | async-done | bytes 98336 | tf_op jit(solution)/shard_map/all_to_all | solution.py:185
  26.7 7.5 %collective-permute-start = (bf16[8,64,768]{2,1,0:T(8,128)(2,1)}, bf16[8,64,768]{2,1,0:T(8,128)(2,1)S(1)}, u32[]{:S(2)}, u32[]{:S(2)}) collective-permute-start(bf16[8,64,768]{2,1,0:T(8,128)(2,1)} %get-tuple-element.16), channel_id=1, source_target_pairs={{0,1},{1,0},{2,3},{3,2},{4,5},{5,4},{6,7},{7,6},{8,9},{9,8},{10,11... | collective-permute-start | bytes 2359304 | tf_op jit(solution)/shard_map/ppermute | solution.py:188
  34.2 0.0 copy-start
  34.2 1.1 %copy-done = bf16[8,64,768]{2,1,0:T(8,128)(2,1)S(1)} copy-done((bf16[8,64,768]{2,1,0:T(8,128)(2,1)S(1)}, bf16[8,64,768]{2,1,0:T(8,128)(2,1)}, u32[]{:S(2)}) %copy-start) | copy-done | bytes 786456
  35.3 0.1 keep.1.own_ref
  35.4 0.9 collective-permute-done.other_ref
  36.3 0.5 fill.1
  36.8 29.3 %all_to_all.15.in_ref.in_hbm = bf16[8,64,1536]{2,1,0:T(8,128)(2,1)S(1)} all-to-all(bf16[8,64,1536]{2,1,0:T(8,128)(2,1)S(1)} %fill.1), channel_id=1, replica_groups={{0,2,64,66,128,130,192,194},{4,6,68,70,132,134,196,198},{8,10,72,74,136..., dimensions={0} | all-to-all | bytes 3145728 | tf_op jit(solution)/shard_map/all_to_all | solution.py:185
  66.1 1.4 %sum.1 = (bf16[64,8,128]{2,1,0:T(8,128)(2,1)}, bf16[2,64,768]{2,1,0:T(8,128)(2,1)S(1)}, bf16[2,64,768]{2,1,0:T(8,128)(2,1)S(1)}, bf16[2,64,768]{2,1,0:T(8,128)(2,1)S(1)}, bf16[2,64,768]{2,1,0:T(8,128)(2,1)S(1)}) custom-call(bf16[8,64,1536]{2,1,0:T(8,128)(2,1)S(1)} %all_to_all.15.in_ref.in_hbm, bf16[8,64,1536]{2,1,0:T(8,128)(2,1)S(1)} %all_to_all.15.in_ref.in_hbm), custom_call_target="tpu_custom_call" | custom-call | flops 1572864 | bytes 2097152 | tf_op jit(solution)/shard_map/sum/pallas_call | solution.py:239
  67.5 7.8 %all-to-all-start.2 = ((bf16[64,8,128]{2,1,0:T(8,128)(2,1)}), bf16[64,8,128]{2,1,0:T(8,128)(2,1)S(1)}, u32[]{:S(2)}, u32[]{:S(2)}) async-start(bf16[64,8,128]{2,1,0:T(8,128)(2,1)} %get-tuple-element.17), calls=%async_computation.2 | async-start | bytes 262144 | tf_op jit(solution)/shard_map/all_to_all | solution.py:185
  75.3 1.9 %collective-permute-start.1 = (bf16[2,64,768]{2,1,0:T(8,128)(2,1)S(1)}, bf16[2,64,768]{2,1,0:T(8,128)(2,1)S(1)}, u32[]{:S(2)}, u32[]{:S(2)}) collective-permute-start(bf16[2,64,768]{2,1,0:T(8,128)(2,1)S(1)} %get-tuple-element.18.refs_0_), channel_id=1, source_target_pairs={{0,1},{1,0},{2,3},{3,2},{4,5},{5,4},{6,7},{7,6},{8,9},{9,8},{10,11... | collective-permute-start | bytes 589832 | tf_op jit(solution)/shard_map/ppermute | solution.py:188
  77.2 2.4 %collective-permute-start.2 = (bf16[2,64,768]{2,1,0:T(8,128)(2,1)S(1)}, bf16[2,64,768]{2,1,0:T(8,128)(2,1)S(1)}, u32[]{:S(2)}, u32[]{:S(2)}) collective-permute-start(bf16[2,64,768]{2,1,0:T(8,128)(2,1)S(1)} %get-tuple-element.19.refs_1_), channel_id=1, source_target_pairs={{0,1},{1,0},{2,3},{3,2},{4,5},{5,4},{6,7},{7,6},{8,9},{9,8},{10,11... | collective-permute-start | bytes 589832 | tf_op jit(solution)/shard_map/ppermute | solution.py:188
  79.6 1.9 %collective-permute-start.3 = (bf16[2,64,768]{2,1,0:T(8,128)(2,1)S(1)}, bf16[2,64,768]{2,1,0:T(8,128)(2,1)S(1)}, u32[]{:S(2)}, u32[]{:S(2)}) collective-permute-start(bf16[2,64,768]{2,1,0:T(8,128)(2,1)S(1)} %get-tuple-element.20.refs_2_), channel_id=1, source_target_pairs={{0,1},{1,0},{2,3},{3,2},{4,5},{5,4},{6,7},{7,6},{8,9},{9,8},{10,11... | collective-permute-start | bytes 589832 | tf_op jit(solution)/shard_map/ppermute | solution.py:188
  81.5 2.4 %collective-permute-start.4 = (bf16[2,64,768]{2,1,0:T(8,128)(2,1)S(1)}, bf16[2,64,768]{2,1,0:T(8,128)(2,1)S(1)}, u32[]{:S(2)}, u32[]{:S(2)}) collective-permute-start(bf16[2,64,768]{2,1,0:T(8,128)(2,1)S(1)} %get-tuple-element.21.refs_3_), channel_id=1, source_target_pairs={{0,1},{1,0},{2,3},{3,2},{4,5},{5,4},{6,7},{7,6},{8,9},{9,8},{10,11... | collective-permute-start | bytes 589832 | tf_op jit(solution)/shard_map/ppermute | solution.py:188
  84.0 0.0 collective-permute-done.1.refs_4_
  84.0 0.0 collective-permute-done.2.refs_5_
  84.0 0.0 collective-permute-done.3.refs_6_
  84.0 1.0 %collective-permute-done.4.refs_7_ = bf16[2,64,768]{2,1,0:T(8,128)(2,1)S(1)} collective-permute-done((bf16[2,64,768]{2,1,0:T(8,128)(2,1)S(1)}, bf16[2,64,768]{2,1,0:T(8,128)(2,1)S(1)}, u32[]{:S(2)}, u32[]{:S(2)}) %collective-permute-start.4) | collective-permute-done | bytes 196640 | tf_op jit(solution)/shard_map/ppermute | solution.py:188
  85.0 4.1 %values.1 = bf16[64,128]{1,0:T(8,128)(2,1)} custom-call(s32[1]{0:T(128)} %bitcast.core_ref, bf16[2,64,768]{2,1,0:T(8,128)(2,1)S(1)} %get-tuple-element.18.refs_0_, bf16[2,64,768]{2,1,0:T(8,128)(2,1)S(1)} %get-tuple-element.19.refs_1_, bf16[2,64,768]{2,1,0:T(8,128)(2,1)S(1)} %get-tuple-element.20.refs_2_, bf16[2,64,768]{2,1,0:T(8,128)(2,1)S(1)} %get-tuple-element.21.refs_3_, ...), custom_call_target="tpu_custom_call" | custom-call | flops 201326592 | bytes 5242880 | tf_op jit(solution)/shard_map/values/pallas_call | solution.py:251
  89.1 1.9 %all-to-all-done.2.in_ref = bf16[64,8,128]{2,1,0:T(8,128)(2,1)S(1)} async-done(((bf16[64,8,128]{2,1,0:T(8,128)(2,1)}), bf16[64,8,128]{2,1,0:T(8,128)(2,1)S(1)}, u32[]{:S(2)}, u32[]{:S(2)}) %all-to-all-start.2) | async-done | bytes 131104 | tf_op jit(solution)/shard_map/all_to_all | solution.py:185
  91.0 0.7 final.1
Async XLA Ops:
  2.1 24.6 %all-to-all-start = ((bf16[16,16,192]{2,1,0:T(8,128)(2,1)}), bf16[16,16,192]{2,1,0:T(8,128)(2,1)S(1)}, u32[]{:S(2)}, u32[]{:S(2)}) async-start(bf16[16,16,192]{2,1,0:T(8,128)(2,1)} %scale.1), calls=%async_computation | async-start | bytes 262144 | tf_op jit(solution)/shard_map/all_to_all | solution.py:185
  26.7 9.6 %collective-permute-start = (bf16[8,64,768]{2,1,0:T(8,128)(2,1)}, bf16[8,64,768]{2,1,0:T(8,128)(2,1)S(1)}, u32[]{:S(2)}, u32[]{:S(2)}) collective-permute-start(bf16[8,64,768]{2,1,0:T(8,128)(2,1)} %get-tuple-element.16), channel_id=1, source_target_pairs={{0,1},{1,0},{2,3},{3,2},{4,5},{5,4},{6,7},{7,6},{8,9},{9,8},{10,11... | collective-permute-start | bytes 2359304 | tf_op jit(solution)/shard_map/ppermute | solution.py:188
  34.2 1.1 %copy-start = (bf16[8,64,768]{2,1,0:T(8,128)(2,1)S(1)}, bf16[8,64,768]{2,1,0:T(8,128)(2,1)}, u32[]{:S(2)}) copy-start(bf16[8,64,768]{2,1,0:T(8,128)(2,1)} %get-tuple-element.15.in_hbm) | copy-start | bytes 2359300
  67.5 23.5 %all-to-all-start.2 = ((bf16[64,8,128]{2,1,0:T(8,128)(2,1)}), bf16[64,8,128]{2,1,0:T(8,128)(2,1)S(1)}, u32[]{:S(2)}, u32[]{:S(2)}) async-start(bf16[64,8,128]{2,1,0:T(8,128)(2,1)} %get-tuple-element.17), calls=%async_computation.2 | async-start | bytes 262144 | tf_op jit(solution)/shard_map/all_to_all | solution.py:185
  75.3 8.7 %collective-permute-start.1 = (bf16[2,64,768]{2,1,0:T(8,128)(2,1)S(1)}, bf16[2,64,768]{2,1,0:T(8,128)(2,1)S(1)}, u32[]{:S(2)}, u32[]{:S(2)}) collective-permute-start(bf16[2,64,768]{2,1,0:T(8,128)(2,1)S(1)} %get-tuple-element.18.refs_0_), channel_id=1, source_target_pairs={{0,1},{1,0},{2,3},{3,2},{4,5},{5,4},{6,7},{7,6},{8,9},{9,8},{10,11... | collective-permute-start | bytes 589832 | tf_op jit(solution)/shard_map/ppermute | solution.py:188
  77.2 6.8 %collective-permute-start.2 = (bf16[2,64,768]{2,1,0:T(8,128)(2,1)S(1)}, bf16[2,64,768]{2,1,0:T(8,128)(2,1)S(1)}, u32[]{:S(2)}, u32[]{:S(2)}) collective-permute-start(bf16[2,64,768]{2,1,0:T(8,128)(2,1)S(1)} %get-tuple-element.19.refs_1_), channel_id=1, source_target_pairs={{0,1},{1,0},{2,3},{3,2},{4,5},{5,4},{6,7},{7,6},{8,9},{9,8},{10,11... | collective-permute-start | bytes 589832 | tf_op jit(solution)/shard_map/ppermute | solution.py:188
  79.6 4.4 %collective-permute-start.3 = (bf16[2,64,768]{2,1,0:T(8,128)(2,1)S(1)}, bf16[2,64,768]{2,1,0:T(8,128)(2,1)S(1)}, u32[]{:S(2)}, u32[]{:S(2)}) collective-permute-start(bf16[2,64,768]{2,1,0:T(8,128)(2,1)S(1)} %get-tuple-element.20.refs_2_), channel_id=1, source_target_pairs={{0,1},{1,0},{2,3},{3,2},{4,5},{5,4},{6,7},{7,6},{8,9},{9,8},{10,11... | collective-permute-start | bytes 589832 | tf_op jit(solution)/shard_map/ppermute | solution.py:188
  81.5 3.5 %collective-permute-start.4 = (bf16[2,64,768]{2,1,0:T(8,128)(2,1)S(1)}, bf16[2,64,768]{2,1,0:T(8,128)(2,1)S(1)}, u32[]{:S(2)}, u32[]{:S(2)}) collective-permute-start(bf16[2,64,768]{2,1,0:T(8,128)(2,1)S(1)} %get-tuple-element.21.refs_3_), channel_id=1, source_target_pairs={{0,1},{1,0},{2,3},{3,2},{4,5},{5,4},{6,7},{7,6},{8,9},{9,8},{10,11... | collective-permute-start | bytes 589832 | tf_op jit(solution)/shard_map/ppermute | solution.py:188
